TPU v7x, 32 devices: a whole 2x2x4 slice. The times are simulated.
32 devices in a mesh: dp: 8 (over y, x, core), mp: 4 (over z).
Axes of the slice: x: 2, y: 2, z: 4, core: 2. Of those that a mesh axis runs over, the one named last changes fastest.
Arguments:
- text_embeds: bfloat16 [4, 16, 40, 768], P(None, 'dp'), may hold values from -6 to 6
- text_lengths: int32 [4, 16], P(None, 'dp'), may hold values from 10 to 40
- image_embeds: bfloat16 [4, 16, 145, 768], P(None, 'dp'), may hold values from -6 to 6
- image_mask: int32 [4, 16, 145], P(None, 'dp'), may hold values from 0 to 1, as said below
- image_ids: int32 [4, 16], replicated, may hold values from 0 to 7
- out_cot: bfloat16 [4, 16, 40, 768], P(None, 'dp', 'mp'), may hold values from -6 to 6
- text_qkv: bfloat16 [3, 768, 768], P(None, 'dp', 'mp'), may hold values from -0.21875 to 0.21875
- text_out: bfloat16 [768, 768], P('mp', 'dp'), may hold values from -0.5 to 0.5
- text_up: bfloat16 [768, 3072], P('dp', 'mp'), may hold values from -0.21875 to 0.21875
- text_down: bfloat16 [3072, 768], P('mp', 'dp'), may hold values from -0.109375 to 0.109375
- merge_qkv: bfloat16 [6, 768, 768], P(None, 'dp', 'mp'), may hold values from -0.21875 to 0.21875
- merge_out: bfloat16 [2, 768, 768], P(None, 'mp', 'dp'), may hold values from -0.625 to 0.625
- merge_up: bfloat16 [768, 3072], P('dp', 'mp'), may hold values from -0.21875 to 0.21875
- merge_down: bfloat16 [3072, 768], P('mp', 'dp'), may hold values from -0.109375 to 0.109375
- projections: bfloat16 [2, 768, 256], P(None, 'dp'), may hold values from -0.21875 to 0.21875
- norm_gains: float32 [5, 768], replicated, may hold values from 0.5 to 1.5
- offsets: float32 [10, 768], replicated, may hold values from -1.2 to 1.2
- head_biases: float32 [6, 768], P(None, 'mp'), may hold values from -1.2 to 1.2
- up_biases: float32 [2, 3072], P(None, 'mp'), may hold values from -1.2 to 1.2
Outputs:
- merged: float32 [4, 16, 40, 768], P(None, 'dp', 'mp')
- pair_loss: float32 [4, 16], P(None, 'dp')
- text_grad: float32 [4, 16, 40, 768], P(None, 'dp', 'mp')
- image_grad: float32 [4, 16, 145, 768], P(None, 'dp', None, 'mp')
- text_qkv_grad: float32 [3, 768, 768], P(None, 'dp', 'mp')
- text_out_grad: float32 [768, 768], P('mp', 'dp')
- text_up_grad: float32 [768, 3072], P('dp', 'mp')
- text_down_grad: float32 [3072, 768], P('mp', 'dp')
- merge_qkv_grad: float32 [6, 768, 768], P(None, 'dp', 'mp')
- merge_out_grad: float32 [2, 768, 768], P(None, 'mp', 'dp')
- merge_up_grad: float32 [768, 3072], P('dp', 'mp')
- merge_down_grad: float32 [3072, 768], P('mp', 'dp')
- projections_grad: float32 [2, 768, 256], P(None, 'dp')
- norm_gains_grad: float32 [5, 768], replicated
- offsets_grad: float32 [10, 768], replicated
- head_biases_grad: float32 [6, 768], P(None, 'mp')
- up_biases_grad: float32 [2, 3072], P(None, 'mp')
Inputs may be any that keep to these rules, and one draw needn't show every extreme that they name: `image_mask`: in each image the first 50 tokens are live and the rest are either all live or all padding; in each micro-batch exactly 8 images are fully live.
All inputs are finite; a program needn't handle non-finite values.
Results may differ from a plain program's by a relative error of at most 0.028.
Values may be sent and summed in bfloat16 or wider, within the bound.
A program may use at most 192 MiB of HBM per device.

v0:
```python
import math

import jax
import jax.numpy as jnp
from jax import lax
from jax.sharding import PartitionSpec as P

HEAD_DIM = 64


EPS = 1e-06
SCORE_SCALE = 0.05
EXACT_DOT_MODE = lax.Precision.HIGHEST
NEGATIVE = -1e30


def layer_norm(before, gain, shift):
    centre = before - jnp.mean(before, -1, keepdims=True)
    second = jnp.mean(centre * centre, -1, keepdims=True)
    return centre * lax.rsqrt(second + EPS) * gain + shift


def unit_rows(raw):
    return raw * lax.rsqrt(jnp.sum(raw * raw, -1, keepdims=True) + EPS)


def gelu_exact(pre):
    return jax.nn.gelu(pre, approximate=False)


def product(left, right):
    return jnp.dot(left, right, preferred_element_type=jnp.float32)


def row_contract(left, right):
    return lax.dot_general(
        left, right, (((0,), (0,)), ((), ())), preferred_element_type=jnp.float32
    )


def column_contract(left, right):
    return lax.dot_general(
        left, right, (((1,), (1,)), ((), ())), preferred_element_type=jnp.float32
    )


def rows_from(source, start, count):
    return lax.dynamic_slice_in_dim(source, start, count, 0)


def out_term(mixed, weight):

    def term(start, count):
        return product(rows_from(mixed, start, count), weight)

    return term


def back_term(grads, weight):

    def term(start, count):
        return column_contract(rows_from(grads, start, count), weight)

    return term


def joined_split(joined_grad, count):
    rows, columns = joined_grad.shape
    return jnp.transpose(joined_grad.reshape(rows, count, columns // count), (1, 0, 2))


def settle(hidden, term, bias, gain, shift):
    share_rows = hidden.shape[0] // lax.axis_size("mp")
    start = lax.axis_index("mp") * share_rows
    summed = lax.psum_scatter(
        term(jnp.int32(0), share_rows * lax.axis_size("mp")), "mp", scatter_dimension=0, tiled=True
    )
    before = rows_from(hidden, start, share_rows).astype(jnp.float32) + summed + bias
    return (before, layer_norm(before, gain, shift))


def spread(share):
    return lax.all_gather(share.astype(jnp.bfloat16), "mp", axis=0, tiled=True)


def unsettle(grad_share, before, gain, shift):
    _, pull = jax.vjp(layer_norm, before, gain, shift)
    grad_before, grad_gain, grad_shift = pull(grad_share)
    rounded = grad_before.astype(jnp.bfloat16)
    grad_bias = jnp.sum(rounded.astype(jnp.float32), 0)
    grad_full = lax.all_gather(rounded, "mp", axis=0, tiled=True)
    return (grad_before, grad_full, grad_gain, grad_shift, grad_bias)


def gather_back(grad_before, term):
    return grad_before + lax.psum_scatter(
        term(jnp.int32(0), grad_before.shape[0] * lax.axis_size("mp")),
        "mp",
        scatter_dimension=0,
        tiled=True,
    )


def attention_forward(queries, keys, values, valid, scale):
    scores = (
        jnp.einsum("qphd,pkhd->phqk", queries, keys, preferred_element_type=jnp.float32) * scale
    )
    scores = jnp.where(valid[:, None, None, :], scores, NEGATIVE)
    highest = jnp.max(scores, -1, keepdims=True)
    raised = jnp.exp(scores - highest)
    totals = jnp.sum(raised, -1, keepdims=True)
    probs = (raised / totals).astype(jnp.bfloat16)
    mixed = jnp.einsum("phqk,pkhd->qphd", probs, values, preferred_element_type=jnp.float32)
    return (mixed.astype(jnp.bfloat16), highest + jnp.log(totals))


def attention_backward(queries, keys, values, valid, log_total, grad_mixed, scale):
    scores = (
        jnp.einsum("qphd,pkhd->phqk", queries, keys, preferred_element_type=jnp.float32) * scale
    )
    scores = jnp.where(valid[:, None, None, :], scores, NEGATIVE)
    probs = jnp.exp(scores - log_total)
    grad_values = jnp.einsum(
        "phqk,qphd->pkhd",
        probs.astype(jnp.bfloat16),
        grad_mixed,
        preferred_element_type=jnp.float32,
    )
    grad_probs = jnp.einsum(
        "qphd,pkhd->phqk", grad_mixed, values, preferred_element_type=jnp.float32
    )
    grad_scores = probs * (grad_probs - jnp.sum(grad_probs * probs, -1, keepdims=True))
    rounded = grad_scores.astype(jnp.bfloat16)
    grad_queries = (
        jnp.einsum("phqk,pkhd->qphd", rounded, keys, preferred_element_type=jnp.float32) * scale
    )
    grad_keys = (
        jnp.einsum("phqk,qphd->pkhd", rounded, queries, preferred_element_type=jnp.float32) * scale
    )
    return (
        grad_queries.astype(jnp.bfloat16),
        grad_keys.astype(jnp.bfloat16),
        grad_values.astype(jnp.bfloat16),
    )


def self_forward(hidden, joined, bias_query, bias_value, valid, pairs, scale):
    local = joined.shape[1] // 3
    heads = local // HEAD_DIM
    made = product(hidden, joined)
    queries = (
        (made[:, :local] + bias_query).astype(jnp.bfloat16).reshape(-1, pairs, heads, HEAD_DIM)
    )
    keys = jnp.swapaxes(
        made[:, local : 2 * local].astype(jnp.bfloat16).reshape(-1, pairs, heads, HEAD_DIM), 0, 1
    )
    values = jnp.swapaxes(
        (made[:, 2 * local :] + bias_value)
        .astype(jnp.bfloat16)
        .reshape(-1, pairs, heads, HEAD_DIM),
        0,
        1,
    )
    mixed, log_total = attention_forward(queries, keys, values, valid, scale)
    return ((queries, keys, values, log_total), mixed.reshape(-1, local))


def self_backward(kept, hidden, mixed, grad_full, joined, weight_out, valid, scale):
    queries, keys, values, log_total = kept
    rows = hidden.shape[0]
    local = mixed.shape[1]
    grad_mixed = column_contract(grad_full, weight_out).astype(jnp.bfloat16).reshape(queries.shape)
    grad_queries, grad_keys, grad_values = attention_backward(
        queries, keys, values, valid, log_total, grad_mixed, scale
    )
    grads = jnp.concatenate(
        [
            grad_queries.reshape(rows, local),
            jnp.swapaxes(grad_keys, 0, 1).reshape(rows, local),
            jnp.swapaxes(grad_values, 0, 1).reshape(rows, local),
        ],
        1,
    )
    joined_grad = row_contract(hidden, grads)
    out_grad = row_contract(mixed, grad_full)
    bias_query = jnp.sum(grads[:, :local].astype(jnp.float32), 0)
    bias_value = jnp.sum(grads[:, 2 * local :].astype(jnp.float32), 0)
    return (back_term(grads, joined), joined_grad, out_grad, bias_query, bias_value)


def cross_forward(
    hidden, image_rows, weight_query, joined, bias_query, bias_value, valid, pairs, scale
):
    local = weight_query.shape[1]
    heads = local // HEAD_DIM
    queries = (
        (product(hidden, weight_query) + bias_query)
        .astype(jnp.bfloat16)
        .reshape(-1, pairs, heads, HEAD_DIM)
    )
    made = product(image_rows, joined)
    keys = made[:, :local].astype(jnp.bfloat16).reshape(pairs, -1, heads, HEAD_DIM)
    values = (made[:, local:] + bias_value).astype(jnp.bfloat16).reshape(pairs, -1, heads, HEAD_DIM)
    mixed, log_total = attention_forward(queries, keys, values, valid, scale)
    return ((queries, keys, values, log_total), mixed.reshape(-1, local))


def cross_backward(
    kept, hidden, image_rows, mixed, grad_full, weight_query, joined, weight_out, valid, scale
):
    queries, keys, values, log_total = kept
    rows = hidden.shape[0]
    local = mixed.shape[1]
    grad_mixed = column_contract(grad_full, weight_out).astype(jnp.bfloat16).reshape(queries.shape)
    grad_queries, grad_keys, grad_values = attention_backward(
        queries, keys, values, valid, log_total, grad_mixed, scale
    )
    query_grads = grad_queries.reshape(rows, local)
    image_grads = jnp.concatenate([grad_keys.reshape(-1, local), grad_values.reshape(-1, local)], 1)
    query_weight_grad = row_contract(hidden, query_grads)
    joined_grad = row_contract(image_rows, image_grads)
    out_grad = row_contract(mixed, grad_full)
    image_part = column_contract(image_grads, joined)
    bias_query = jnp.sum(query_grads.astype(jnp.float32), 0)
    bias_value = jnp.sum(image_grads[:, local:].astype(jnp.float32), 0)
    return (
        back_term(query_grads, weight_query),
        image_part,
        query_weight_grad,
        joined_grad,
        out_grad,
        bias_query,
        bias_value,
    )


def ffn_forward(hidden, weight_up, bias_up):
    pre = product(hidden, weight_up) + bias_up
    return (pre, gelu_exact(pre).astype(jnp.bfloat16))


def ffn_backward(hidden, pre, active, grad_full, weight_up, weight_down):
    grad_active = column_contract(grad_full, weight_down)
    _, pull = jax.vjp(gelu_exact, pre)
    grad_pre = pull(grad_active)[0].astype(jnp.bfloat16)
    down_grad = row_contract(active, grad_full)
    up_grad = row_contract(hidden, grad_pre)
    bias_grad = jnp.sum(grad_pre.astype(jnp.float32), 0)
    return (back_term(grad_pre, weight_up), up_grad, down_grad, bias_grad)


def contrast(text_cls, image_cls, text_proj, image_proj, own_ids, all_ids):
    caption_normed_embedding, text_pull = jax.vjp(unit_rows, product(text_cls, text_proj))
    picture_normed_embedding, image_pull = jax.vjp(unit_rows, product(image_cls, image_proj))
    gathered_text_features, gathered_image_features = (
        lax.all_gather(caption_normed_embedding, "dp", axis=0, tiled=True),
        lax.all_gather(picture_normed_embedding, "dp", axis=0, tiled=True),
    )
    same = (own_ids[:, None] == all_ids[None, :]).astype(jnp.float32)
    paired_target_index = same / jnp.sum(same, 1, keepdims=True)
    caption_row_logsoftmax = jax.nn.log_softmax(
        jnp.dot(caption_normed_embedding, gathered_image_features.T, precision=EXACT_DOT_MODE)
        / SCORE_SCALE,
        axis=1,
    )
    picture_row_logsoftmax = jax.nn.log_softmax(
        jnp.dot(picture_normed_embedding, gathered_text_features.T, precision=EXACT_DOT_MODE)
        / SCORE_SCALE,
        axis=1,
    )
    loss = -0.5 * (
        jnp.sum(paired_target_index * caption_row_logsoftmax, 1)
        + jnp.sum(paired_target_index * picture_row_logsoftmax, 1)
    )
    caption_score_excess = (
        0.5 * (jnp.exp(caption_row_logsoftmax) - paired_target_index) / SCORE_SCALE
    )
    picture_score_excess = (
        0.5 * (jnp.exp(picture_row_logsoftmax) - paired_target_index) / SCORE_SCALE
    )
    grad_text_own = jnp.dot(caption_score_excess, gathered_image_features, precision=EXACT_DOT_MODE)
    grad_image_own = jnp.dot(picture_score_excess, gathered_text_features, precision=EXACT_DOT_MODE)
    grad_all_image = jnp.dot(
        caption_score_excess.T, caption_normed_embedding, precision=EXACT_DOT_MODE
    )
    grad_all_text = jnp.dot(
        picture_score_excess.T, picture_normed_embedding, precision=EXACT_DOT_MODE
    )
    back_text, back_image = (
        lax.psum_scatter(grad_all_text, "dp", scatter_dimension=0, tiled=True),
        lax.psum_scatter(grad_all_image, "dp", scatter_dimension=0, tiled=True),
    )
    text_feature = grad_text_own + back_text
    image_feature = grad_image_own + back_image
    text_raw_grad = text_pull(text_feature)[0]
    image_raw_grad = image_pull(image_feature)[0]
    text_proj_grad = jnp.dot(
        text_cls.astype(jnp.float32).T, text_raw_grad, precision=EXACT_DOT_MODE
    )
    image_proj_grad = jnp.dot(
        image_cls.astype(jnp.float32).T, image_raw_grad, precision=EXACT_DOT_MODE
    )
    text_cls_grad = jnp.dot(
        text_raw_grad, text_proj.astype(jnp.float32).T, precision=EXACT_DOT_MODE
    )
    image_cls_grad = jnp.dot(
        image_raw_grad, image_proj.astype(jnp.float32).T, precision=EXACT_DOT_MODE
    )
    return (loss, text_cls_grad, image_cls_grad, text_proj_grad, image_proj_grad)


def shards(
    text_embeds,
    text_lengths,
    image_embeds,
    image_mask,
    image_ids,
    out_cot,
    text_qkv,
    text_out,
    text_up,
    text_down,
    merge_qkv,
    merge_out,
    merge_up,
    merge_down,
    projections,
    norm_gains,
    offsets,
    head_biases,
    up_biases,
):
    (
        text_qkv_all,
        text_out_all,
        text_up_all,
        text_down_all,
        merge_qkv_all,
        merge_out_all,
        merge_up_all,
        merge_down_all,
        projections_all,
    ) = (
        lax.all_gather(text_qkv, "dp", axis=1, tiled=True),
        lax.all_gather(text_out, "dp", axis=1, tiled=True),
        lax.all_gather(text_up, "dp", axis=0, tiled=True),
        lax.all_gather(text_down, "dp", axis=1, tiled=True),
        lax.all_gather(merge_qkv, "dp", axis=1, tiled=True),
        lax.all_gather(merge_out, "dp", axis=2, tiled=True),
        lax.all_gather(merge_up, "dp", axis=0, tiled=True),
        lax.all_gather(merge_down, "dp", axis=1, tiled=True),
        lax.all_gather(projections, "dp", axis=1, tiled=True),
    )
    text_joined = jnp.concatenate([text_qkv_all[0], text_qkv_all[1], text_qkv_all[2]], 1)
    self_joined = jnp.concatenate([merge_qkv_all[0], merge_qkv_all[1], merge_qkv_all[2]], 1)
    cross_joined = jnp.concatenate([merge_qkv_all[4], merge_qkv_all[5]], 1)
    micro, pairs, tokens, width = text_embeds.shape
    images = image_embeds.shape[2]
    local = text_qkv_all.shape[2]
    hidden_local = text_up_all.shape[1]
    model_parts = lax.axis_size("mp")
    model_index = lax.axis_index("mp")
    data_index = lax.axis_index("dp")
    scale = 1.0 / math.sqrt(HEAD_DIM)
    first_share = (model_index == 0).astype(jnp.float32)
    text_joined_grad = jnp.zeros((width, 3 * local), jnp.float32)
    text_out_grad = jnp.zeros((local, width), jnp.float32)
    text_up_grad = jnp.zeros((width, hidden_local), jnp.float32)
    text_down_grad = jnp.zeros((hidden_local, width), jnp.float32)
    self_joined_grad = jnp.zeros((width, 3 * local), jnp.float32)
    cross_query_grad = jnp.zeros((width, local), jnp.float32)
    cross_joined_grad = jnp.zeros((width, 2 * local), jnp.float32)
    self_out_grad = jnp.zeros((local, width), jnp.float32)
    cross_out_grad = jnp.zeros((local, width), jnp.float32)
    merge_up_grad = jnp.zeros((width, hidden_local), jnp.float32)
    merge_down_grad = jnp.zeros((hidden_local, width), jnp.float32)
    text_proj_total = jnp.zeros(projections_all.shape[1:], jnp.float32)
    image_proj_total = jnp.zeros(projections_all.shape[1:], jnp.float32)
    gain_list = [jnp.zeros((width,), jnp.float32) for place in range(5)]
    offset_list = [jnp.zeros((width,), jnp.float32) for place in range(10)]
    head_list = [jnp.zeros((local,), jnp.float32) for place in range(6)]
    up_list = [jnp.zeros((hidden_local,), jnp.float32) for place in range(2)]
    merged_list, loss_list, text_list, image_list = ([], [], [], [])
    for step in range(micro):
        hidden0 = jnp.swapaxes(text_embeds[step], 0, 1).reshape(tokens * pairs, width)
        image_rows = image_embeds[step].reshape(pairs * images, width)
        text_valid = (
            lax.broadcasted_iota(jnp.int32, (pairs, tokens), 1) < text_lengths[step][:, None]
        )
        image_valid = image_mask[step] > 0
        kept0, mixed0 = self_forward(
            hidden0, text_joined, head_biases[0], head_biases[1], text_valid, pairs, scale
        )
        before0, share1 = settle(
            hidden0, out_term(mixed0, text_out_all), offsets[0], norm_gains[0], offsets[5]
        )
        hidden1 = spread(share1)
        pre1, active1 = ffn_forward(hidden1, text_up_all, up_biases[0])
        before1, share2 = settle(
            hidden1, out_term(active1, text_down_all), offsets[1], norm_gains[1], offsets[6]
        )
        hidden2 = spread(share2)
        all_ids = image_ids[step]
        own_start = data_index * pairs
        own_ids = lax.dynamic_slice_in_dim(all_ids, own_start, pairs, 0)
        loss, text_cls_grad, image_cls_grad, text_proj_grad, image_proj_grad = contrast(
            hidden2[:pairs],
            image_embeds[step][:, 0],
            projections_all[0],
            projections_all[1],
            own_ids,
            all_ids,
        )
        loss_list.append(loss)
        text_proj_total = text_proj_total + text_proj_grad
        image_proj_total = image_proj_total + image_proj_grad
        kept2, mixed2 = self_forward(
            hidden2, self_joined, head_biases[2], head_biases[3], text_valid, pairs, scale
        )
        before2, share3 = settle(
            hidden2, out_term(mixed2, merge_out_all[0]), offsets[2], norm_gains[2], offsets[7]
        )
        hidden3 = spread(share3)
        kept3, mixed3 = cross_forward(
            hidden3,
            image_rows,
            merge_qkv_all[3],
            cross_joined,
            head_biases[4],
            head_biases[5],
            image_valid,
            pairs,
            scale,
        )
        before3, share4 = settle(
            hidden3, out_term(mixed3, merge_out_all[1]), offsets[3], norm_gains[3], offsets[8]
        )
        hidden4 = spread(share4)
        pre4, active4 = ffn_forward(hidden4, merge_up_all, up_biases[1])
        before4, out_share = settle(
            hidden4, out_term(active4, merge_down_all), offsets[4], norm_gains[4], offsets[9]
        )
        share_tokens = out_share.shape[0] // pairs
        merged_list.append(jnp.swapaxes(out_share.reshape(share_tokens, pairs, width), 0, 1))
        cot_rows = jnp.swapaxes(out_cot[step], 0, 1).reshape(-1, width).astype(jnp.float32)
        grad_before, grad_full, grad_gain, grad_shift, grad_bias = unsettle(
            cot_rows, before4, norm_gains[4], offsets[9]
        )
        gain_list[4] = gain_list[4] + grad_gain
        offset_list[9] = offset_list[9] + grad_shift
        offset_list[4] = offset_list[4] + grad_bias
        term, up_grad, down_grad, bias_up = ffn_backward(
            hidden4, pre4, active4, grad_full, merge_up_all, merge_down_all
        )
        merge_up_grad = merge_up_grad + up_grad
        merge_down_grad = merge_down_grad + down_grad
        up_list[1] = up_list[1] + bias_up
        grad_hidden4 = gather_back(grad_before, term)
        grad_before, grad_full, grad_gain, grad_shift, grad_bias = unsettle(
            grad_hidden4, before3, norm_gains[3], offsets[8]
        )
        gain_list[3] = gain_list[3] + grad_gain
        offset_list[8] = offset_list[8] + grad_shift
        offset_list[3] = offset_list[3] + grad_bias
        term, image_part, query_grad, joined_grad, out_grad, bias_query, bias_value = (
            cross_backward(
                kept3,
                hidden3,
                image_rows,
                mixed3,
                grad_full,
                merge_qkv_all[3],
                cross_joined,
                merge_out_all[1],
                image_valid,
                scale,
            )
        )
        cross_query_grad = cross_query_grad + query_grad
        cross_joined_grad = cross_joined_grad + joined_grad
        cross_out_grad = cross_out_grad + out_grad
        head_list[4] = head_list[4] + bias_query
        head_list[5] = head_list[5] + bias_value
        image_share = lax.psum_scatter(image_part, "mp", scatter_dimension=1, tiled=True).reshape(
            pairs, images, local
        )
        cls_part = lax.dynamic_slice_in_dim(image_cls_grad, model_index * local, local, 1)
        image_list.append(
            jnp.concatenate([image_share[:, :1] + cls_part[:, None], image_share[:, 1:]], 1)
        )
        grad_hidden3 = gather_back(grad_before, term)
        grad_before, grad_full, grad_gain, grad_shift, grad_bias = unsettle(
            grad_hidden3, before2, norm_gains[2], offsets[7]
        )
        gain_list[2] = gain_list[2] + grad_gain
        offset_list[7] = offset_list[7] + grad_shift
        offset_list[2] = offset_list[2] + grad_bias
        term, joined_grad, out_grad, bias_query, bias_value = self_backward(
            kept2, hidden2, mixed2, grad_full, self_joined, merge_out_all[0], text_valid, scale
        )
        self_joined_grad = self_joined_grad + joined_grad
        self_out_grad = self_out_grad + out_grad
        head_list[2] = head_list[2] + bias_query
        head_list[3] = head_list[3] + bias_value
        grad_hidden2 = gather_back(grad_before, term)
        extra = jnp.concatenate(
            [text_cls_grad, jnp.zeros((grad_hidden2.shape[0] - pairs, width), jnp.float32)], 0
        )
        grad_hidden2 = grad_hidden2 + extra * first_share
        grad_before, grad_full, grad_gain, grad_shift, grad_bias = unsettle(
            grad_hidden2, before1, norm_gains[1], offsets[6]
        )
        gain_list[1] = gain_list[1] + grad_gain
        offset_list[6] = offset_list[6] + grad_shift
        offset_list[1] = offset_list[1] + grad_bias
        term, up_grad, down_grad, bias_up = ffn_backward(
            hidden1, pre1, active1, grad_full, text_up_all, text_down_all
        )
        text_up_grad = text_up_grad + up_grad
        text_down_grad = text_down_grad + down_grad
        up_list[0] = up_list[0] + bias_up
        grad_hidden1 = gather_back(grad_before, term)
        grad_before, grad_full, grad_gain, grad_shift, grad_bias = unsettle(
            grad_hidden1, before0, norm_gains[0], offsets[5]
        )
        gain_list[0] = gain_list[0] + grad_gain
        offset_list[5] = offset_list[5] + grad_shift
        offset_list[0] = offset_list[0] + grad_bias
        term, joined_grad, out_grad, bias_query, bias_value = self_backward(
            kept0, hidden0, mixed0, grad_full, text_joined, text_out_all, text_valid, scale
        )
        text_joined_grad = text_joined_grad + joined_grad
        text_out_grad = text_out_grad + out_grad
        head_list[0] = head_list[0] + bias_query
        head_list[1] = head_list[1] + bias_value
        grad_hidden0 = gather_back(grad_before, term)
        text_list.append(jnp.swapaxes(grad_hidden0.reshape(share_tokens, pairs, width), 0, 1))
    head_full = lax.dynamic_update_slice_in_dim(
        jnp.zeros((6, width), jnp.float32), jnp.stack(head_list), model_index * local, 1
    )
    up_full = lax.dynamic_update_slice_in_dim(
        jnp.zeros((2, hidden_local * model_parts), jnp.float32),
        jnp.stack(up_list),
        model_index * hidden_local,
        1,
    )
    gains_sum, offsets_sum, heads_sum, ups_sum = lax.psum(
        (jnp.stack(gain_list), jnp.stack(offset_list), head_full, up_full), ("dp", "mp")
    )
    head_out = lax.dynamic_slice_in_dim(heads_sum, model_index * local, local, 1)
    up_out = lax.dynamic_slice_in_dim(ups_sum, model_index * hidden_local, hidden_local, 1)
    text_qkv_grad = joined_split(text_joined_grad, 3)
    projections_grad = jnp.stack([text_proj_total, image_proj_total])
    merging_qkv_grad = jnp.concatenate(
        [
            joined_split(self_joined_grad, 3),
            cross_query_grad[None],
            joined_split(cross_joined_grad, 2),
        ],
        0,
    )
    merging_out_grad = jnp.stack([self_out_grad, cross_out_grad])
    (
        text_qkv_done,
        text_out_done,
        text_up_done,
        text_down_done,
        projections_done,
        merge_qkv_done,
        merge_out_done,
        merge_up_done,
        merge_down_done,
    ) = (
        lax.psum_scatter(text_qkv_grad, "dp", scatter_dimension=1, tiled=True),
        lax.psum_scatter(text_out_grad, "dp", scatter_dimension=1, tiled=True),
        lax.psum_scatter(text_up_grad, "dp", scatter_dimension=0, tiled=True),
        lax.psum_scatter(text_down_grad, "dp", scatter_dimension=1, tiled=True),
        lax.psum_scatter(projections_grad, "dp", scatter_dimension=1, tiled=True),
        lax.psum_scatter(merging_qkv_grad, "dp", scatter_dimension=1, tiled=True),
        lax.psum_scatter(merging_out_grad, "dp", scatter_dimension=2, tiled=True),
        lax.psum_scatter(merge_up_grad, "dp", scatter_dimension=0, tiled=True),
        lax.psum_scatter(merge_down_grad, "dp", scatter_dimension=1, tiled=True),
    )
    return (
        jnp.stack(merged_list),
        jnp.stack(loss_list),
        jnp.stack(text_list),
        jnp.stack(image_list),
        text_qkv_done,
        text_out_done,
        text_up_done,
        text_down_done,
        merge_qkv_done,
        merge_out_done,
        merge_up_done,
        merge_down_done,
        projections_done,
        gains_sum,
        offsets_sum,
        head_out,
        up_out,
    )


def solution(mesh):
    placed = (
        P(None, "dp", None, None),
        P(None, "dp"),
        P(None, "dp", None, None),
        P(None, "dp", None),
        P(),
        P(None, "dp", "mp", None),
        P(None, "dp", "mp"),
        P("mp", "dp"),
        P("dp", "mp"),
        P("mp", "dp"),
        P(None, "dp", "mp"),
        P(None, "mp", "dp"),
        P("dp", "mp"),
        P("mp", "dp"),
        P(None, "dp", None),
        P(),
        P(),
        P(None, "mp"),
        P(None, "mp"),
    )
    return jax.shard_map(
        shards,
        mesh=mesh,
        in_specs=placed,
        out_specs=(
            P(None, "dp", "mp", None),
            P(None, "dp"),
            P(None, "dp", "mp", None),
            P(None, "dp", None, "mp"),
            P(None, "dp", "mp"),
            P("mp", "dp"),
            P("dp", "mp"),
            P("mp", "dp"),
            P(None, "dp", "mp"),
            P(None, "mp", "dp"),
            P("dp", "mp"),
            P("mp", "dp"),
            P(None, "dp", None),
            P(),
            P(),
            P(None, "mp"),
            P(None, "mp"),
        ),
        check_vma=False,
    )
```

profile of v0, /device:TPU:0, one launch (start us, length us, event | category | flops | bytes accessed | tf_op | source)
XLA Modules:
  0.0 2070.4 jit_solution(499638887453136142)
XLA Ops:
  13.2 14.6 all_gather.159
  46.7 26.1 %fusion.662 = (f32[24,768]{1,0:T(8,128)S(1)}, f32[24,768]{1,0:T(8,128)S(1)}, f32[24,768]{1,0:T(8,128)S(1)}, f32[24,768]{1,0:T(8,128)S(1)}) fusion(f32[80,768]{1,0:T(8,128)S(1)} %fusion.782, f32[80,768]{1,0:T(8,128)S(1)} %fusion.778, f32[80,768]{1,0:T(8,128)S(1)} %fusion.774, f32[80,768]{1,0:T(8,128)S(1)} %fusion.770), kind=kCustom, calls=%all-reduce-scatter.49 | all-reduce-scatter fusion | flops 294913 | bytes 1278464
  86.1 11.6 all_gather.183
  113.3 13.5 all-gather
  127.5 13.5 all-gather.4
  141.8 13.8 all-gather.8
  155.6 13.4 all-gather.12
  183.1 17.6 fusion.661
  250.2 13.5 all-gather.1
  273.0 13.5 all-gather.5
  297.3 13.5 all-gather.9
  319.5 13.5 all-gather.13
  402.5 13.2 all-reduce.109.cloned.1.call-done
  425.7 20.3 all-gather.54.cloned.1.call-done
  485.2 26.9 %fusion.660 = (f32[24,768]{1,0:T(8,128)S(1)}, f32[24,768]{1,0:T(8,128)}, f32[24,768]{1,0:T(8,128)}, f32[24,768]{1,0:T(8,128)}) fusion(f32[80,768]{1,0:T(8,128)} %fusion.153, f32[80,768]{1,0:T(8,128)} %fusion.155, f32[80,768]{1,0:T(8,128)} %fusion.157, f32[80,768]{1,0:T(8,128)} %fusion.159), kind=kCustom, calls=%all-reduce-scatter.47 | all-reduce-scatter fusion | flops 294913 | bytes 1278464
  554.4 14.2 all-gather.2
  571.5 14.3 all-gather.6
  589.4 14.2 all-gather.10
  607.2 13.4 all-gather.14
  637.3 17.9 fusion.659
  670.6 13.5 all-gather.3
  684.8 13.5 all-gather.7
  699.0 13.4 all-gather.11
  712.4 14.1 all-gather.15
  742.1 20.4 fusion.658
  796.1 14.1 all-gather.39
  812.8 14.1 all-gather.24
  829.5 14.9 all-gather.29
  846.9 14.2 all-gather.34
  871.1 18.6 fusion.657
  921.0 13.5 all-gather.40
  938.9 14.5 all-gather.25
  961.8 14.2 all-gather.30
  986.5 14.2 all-gather.35
  1027.5 18.4 fusion.656
  1079.2 13.6 all-gather.41
  1100.1 14.2 all-gather.26
  1121.9 13.9 all-gather.31
  1141.3 13.5 all-gather.36
  1168.3 18.1 fusion.655
  1207.5 13.4 all-gather.32
  1221.1 13.7 all-gather.42
  1234.9 13.4 all-gather.27
  1248.4 13.4 all-gather.37
  1267.6 21.1 %fusion.654 = (f32[24,768]{1,0:T(8,128)S(1)}, f32[24,768]{1,0:T(8,128)S(1)}, f32[24,768]{1,0:T(8,128)S(1)}, f32[24,768]{1,0:T(8,128)S(1)}) fusion(f32[80,768]{1,0:T(8,128)S(1)} %fusion.793, f32[80,768]{1,0:T(8,128)S(1)} %fusion.791, f32[80,768]{1,0:T(8,128)S(1)} %fusion.789, f32[80,768]{1,0:T(8,128)S(1)} %fusion.787), kind=kCustom, calls=%all-reduce-scatter.41 | all-reduce-scatter fusion | flops 294913 | bytes 1278464
  1304.2 13.4 all-gather.43
  1318.9 13.4 all-gather.28
  1333.7 13.4 all-gather.33
  1348.9 13.6 all-gather.38
  1373.8 18.8 fusion.653
  1500.8 28.2 %all-reduce.107.cloned.1.call-done = (f32[5,768]{1,0:T(8,128)}, f32[10,768]{1,0:T(8,128)}, f32[6,768]{1,0:T(8,128)}, f32[2,3072]{1,0:T(2,128)}) async-done(((f32[5,768]{1,0:T(8,128)}, f32[10,768]{1,0:T(8,128)}, f32[6,768]{1,0:T(8,128)}, f32[2,3072]{1,0:T(2,128)}), (f32[5,768]{1,0:T(8,128)}, f32[10,768]{1,0:T(8,128)}, f32[6,768]{1,0:T(8,128)}, f32[2,3072]{1,0:T(2,128)})) %all-reduce.107.cloned.1.call-update) | async-done | bytes 89104 | tf_op jit(solution)/shard_map/psum | solution.py:547
  1531.7 35.7 %reduce-scatter.120.cloned.1.call-done = f32[96,192]{1,0:T(8,128)} async-done(((f32[768,192]{1,0:T(8,128)}), f32[96,192]{1,0:T(8,128)}) %reduce-scatter.120.cloned.1.call-update) | async-done | bytes 73744
  1569.1 30.6 %reduce-scatter.104.cloned.1.call-done = f32[290,192]{0,1:T(8,128)} async-done(((f32[290,768]{0,1:T(8,128)}), f32[290,192]{0,1:T(8,128)}) %reduce-scatter.104.cloned.1.call-update) | async-done | bytes 222736 | tf_op jit(solution)/shard_map/reduce_scatter | solution.py:484
  1600.8 29.0 %reduce-scatter.102.cloned.1.call-done = f32[290,192]{0,1:T(8,128)} async-done(((f32[290,768]{0,1:T(8,128)}), f32[290,192]{0,1:T(8,128)}) %reduce-scatter.102.cloned.1.call-update) | async-done | bytes 222736 | tf_op jit(solution)/shard_map/reduce_scatter | solution.py:484
  1631.0 29.2 %reduce-scatter.100.cloned.1.call-done = f32[290,192]{0,1:T(8,128)} async-done(((f32[290,768]{0,1:T(8,128)}), f32[290,192]{0,1:T(8,128)}) %reduce-scatter.100.cloned.1.call-update) | async-done | bytes 222736 | tf_op jit(solution)/shard_map/reduce_scatter | solution.py:484
  1661.4 29.0 %reduce-scatter.98.cloned.1.call-done = f32[290,192]{0,1:T(8,128)} async-done(((f32[290,768]{0,1:T(8,128)}), f32[290,192]{0,1:T(8,128)}) %reduce-scatter.98.cloned.1.call-update) | async-done | bytes 222736 | tf_op jit(solution)/shard_map/reduce_scatter | solution.py:484
  1693.5 35.9 %reduce-scatter.122.cloned.1.call-done = f32[96,384]{1,0:T(8,128)} async-done(((f32[768,384]{1,0:T(8,128)}), f32[96,384]{1,0:T(8,128)}) %reduce-scatter.122.cloned.1.call-update) | async-done | bytes 147472
  1731.4 40.3 %reduce-scatter.118.cloned.1.call-done = f32[2,96,256]{2,1,0:T(8,128)} async-done(((f32[2,768,256]{2,1,0:T(8,128)}), f32[2,96,256]{2,1,0:T(8,128)}) %reduce-scatter.118.cloned.1.call-update) | async-done | bytes 196624 | tf_op jit(solution)/shard_map/reduce_scatter | solution.py:578
  1771.7 46.3 %reduce-scatter.106.cloned.1.call-done = f32[3,96,192]{2,1,0:T(8,128)} async-done(((f32[3,768,192]{2,1,0:T(8,128)}), f32[3,96,192]{2,1,0:T(8,128)}) %reduce-scatter.106.cloned.1.call-update) | async-done | bytes 221200 | tf_op jit(solution)/shard_map/reduce_scatter | solution.py:574
  1818.0 46.6 %reduce-scatter.114.cloned.1.call-done = f32[96,768]{1,0:T(8,128)} async-done(((f32[768,768]{1,0:T(8,128)}), f32[96,768]{1,0:T(8,128)}) %reduce-scatter.114.cloned.1.call-update) | async-done | bytes 294928 | tf_op jit(solution)/shard_map/reduce_scatter | solution.py:581
  1864.6 46.3 %reduce-scatter.116.cloned.1.call-done = f32[768,96]{0,1:T(8,128)} async-done(((f32[768,768]{0,1:T(8,128)}), f32[768,96]{0,1:T(8,128)}) %reduce-scatter.116.cloned.1.call-update) | async-done | bytes 294928 | tf_op jit(solution)/shard_map/reduce_scatter | solution.py:582
  1910.9 46.6 %reduce-scatter.108.cloned.1.call-done = f32[96,768]{1,0:T(8,128)} async-done(((f32[768,768]{1,0:T(8,128)}), f32[96,768]{1,0:T(8,128)}) %reduce-scatter.108.cloned.1.call-update) | async-done | bytes 294928 | tf_op jit(solution)/shard_map/reduce_scatter | solution.py:576
  1957.5 46.4 %reduce-scatter.110.cloned.1.call-done = f32[768,96]{0,1:T(8,128)} async-done(((f32[768,768]{0,1:T(8,128)}), f32[768,96]{0,1:T(8,128)}) %reduce-scatter.110.cloned.1.call-update) | async-done | bytes 294928 | tf_op jit(solution)/shard_map/reduce_scatter | solution.py:577
  2003.9 58.2 %reduce-scatter.112.cloned.1.call-done = f32[6,96,192]{2,1,0:T(8,128)} async-done(((f32[6,768,192]{2,1,0:T(8,128)}), f32[6,96,192]{2,1,0:T(8,128)}) %reduce-scatter.112.cloned.1.call-update) | async-done | bytes 442384 | tf_op jit(solution)/shard_map/reduce_scatter | solution.py:579
  (2667 shorter events, 734.4 us)
Async XLA Ops:
  7.2 161.9 %all-gather.50.cloned.1.call-start = ((), (), s32[]{:S(2)}) async-start(), calls=%async_computation.13 | async-start | bytes 1327104 | tf_op jit(solution)/shard_map/all_gather | solution.py:346
  7.9 165.7 %all-gather.52.cloned.1.call-start = ((), (), s32[]{:S(2)}) async-start(), calls=%async_computation.14 | async-start | bytes 1327104 | tf_op jit(solution)/shard_map/all_gather | solution.py:347
  72.9 38.2 %collective-permute-start = (f32[12,768]{1,0:T(8,128)S(1)}, f32[12,768]{1,0:T(8,128)S(1)}, u32[]{:S(2)}, u32[]{:S(2)}) collective-permute-start(f32[12,768]{1,0:T(8,128)S(1)} %slice.625), channel_id=1, source_target_pairs={{0,1},{1,2},{2,3},{4,5},{5,6},{6,7},{8,9},{9,10},{10,11},{12,13},{... | collective-permute-start | bytes 110600
  76.5 34.7 %collective-permute-start.5 = (f32[12,768]{1,0:T(8,128)S(1)}, f32[12,768]{1,0:T(8,128)S(1)}, u32[]{:S(2)}, u32[]{:S(2)}) collective-permute-start(f32[12,768]{1,0:T(8,128)S(1)} %slice.630), channel_id=1, source_target_pairs={{0,1},{1,2},{2,3},{4,5},{5,6},{6,7},{8,9},{9,10},{10,11},{12,13},{... | collective-permute-start | bytes 110600
  78.4 33.0 %collective-permute-start.10 = (f32[12,768]{1,0:T(8,128)S(1)}, f32[12,768]{1,0:T(8,128)S(1)}, u32[]{:S(2)}, u32[]{:S(2)}) collective-permute-start(f32[12,768]{1,0:T(8,128)S(1)} %slice.635), channel_id=1, source_target_pairs={{0,1},{1,2},{2,3},{4,5},{5,6},{6,7},{8,9},{9,10},{10,11},{12,13},{... | collective-permute-start | bytes 110600
  81.4 30.3 %collective-permute-start.15 = (f32[12,768]{1,0:T(8,128)S(1)}, f32[12,768]{1,0:T(8,128)S(1)}, u32[]{:S(2)}, u32[]{:S(2)}) collective-permute-start(f32[12,768]{1,0:T(8,128)S(1)} %slice.640), channel_id=1, source_target_pairs={{0,1},{1,2},{2,3},{4,5},{5,6},{6,7},{8,9},{9,10},{10,11},{12,13},{... | collective-permute-start | bytes 110600
  83.3 332.4 %all-reduce.109.cloned.1.call-start = ((), (), s32[]{:S(2)}) async-start(), calls=%async_computation.32 | async-start | bytes 262144
  97.6 326.4 %copy-start.10 = (bf16[2,768,256]{2,1,0:T(8,128)(2,1)}, bf16[2,768,256]{2,1,0:T(8,128)(2,1)S(1)}, u32[]{:S(2)}) copy-start(bf16[2,768,256]{2,1,0:T(8,128)(2,1)S(1)} %all_gather.183) | copy-start | bytes 2359300
  102.4 259.7 %copy-start.405 = (f32[2,256]{1,0:T(2,128)}, f32[2,256]{1,0:T(2,128)S(1)}, u32[]{:S(2)}) copy-start(f32[2,256]{1,0:T(2,128)S(1)} %get-tuple-element.678) | copy-start | bytes 6148
  200.7 44.9 %collective-permute-start.1 = (f32[12,768]{1,0:T(8,128)S(1)}, f32[12,768]{1,0:T(8,128)S(1)}, u32[]{:S(2)}, u32[]{:S(2)}) collective-permute-start(f32[12,768]{1,0:T(8,128)S(1)} %slice.626), channel_id=1, source_target_pairs={{0,1},{1,2},{2,3},{4,5},{5,6},{6,7},{8,9},{9,10},{10,11},{12,13},{... | collective-permute-start | bytes 110600
  203.7 42.1 %collective-permute-start.6 = (f32[12,768]{1,0:T(8,128)S(1)}, f32[12,768]{1,0:T(8,128)S(1)}, u32[]{:S(2)}, u32[]{:S(2)}) collective-permute-start(f32[12,768]{1,0:T(8,128)S(1)} %slice.631), channel_id=1, source_target_pairs={{0,1},{1,2},{2,3},{4,5},{5,6},{6,7},{8,9},{9,10},{10,11},{12,13},{... | collective-permute-start | bytes 110600
  206.6 39.4 %collective-permute-start.11 = (f32[12,768]{1,0:T(8,128)S(1)}, f32[12,768]{1,0:T(8,128)S(1)}, u32[]{:S(2)}, u32[]{:S(2)}) collective-permute-start(f32[12,768]{1,0:T(8,128)S(1)} %slice.636), channel_id=1, source_target_pairs={{0,1},{1,2},{2,3},{4,5},{5,6},{6,7},{8,9},{9,10},{10,11},{12,13},{... | collective-permute-start | bytes 110600
  209.2 37.0 %collective-permute-start.16 = (f32[12,768]{1,0:T(8,128)S(1)}, f32[12,768]{1,0:T(8,128)S(1)}, u32[]{:S(2)}, u32[]{:S(2)}) collective-permute-start(f32[12,768]{1,0:T(8,128)S(1)} %slice.641), channel_id=1, source_target_pairs={{0,1},{1,2},{2,3},{4,5},{5,6},{6,7},{8,9},{9,10},{10,11},{12,13},{... | collective-permute-start | bytes 110600
  363.7 82.2 %all-gather.54.cloned.1.call-start = ((), (), s32[]{:S(2)}) async-start(), calls=%async_computation.15 | async-start | bytes 2654208 | tf_op jit(solution)/shard_map/all_gather | solution.py:348
  364.3 362.3 %all-gather.56.cloned.1.call-start = ((), (), s32[]{:S(2)}) async-start(), calls=%async_computation.16 | async-start | bytes 1327104 | tf_op jit(solution)/shard_map/all_gather | solution.py:350
  364.9 366.3 %all-gather.58.cloned.1.call-start = ((), (), s32[]{:S(2)}) async-start(), calls=%async_computation.17 | async-start | bytes 1327104 | tf_op jit(solution)/shard_map/all_gather | solution.py:351
  365.6 1163.5 %all-reduce.107.cloned.1.call-start = ((), (), s32[]{:S(2)}) async-start(), calls=%async_computation.31 | async-start | bytes 245760 | tf_op jit(solution)/shard_map/psum | solution.py:547
  516.9 24.0 %collective-permute-start.2 = (f32[12,768]{1,0:T(8,128)}, f32[12,768]{1,0:T(8,128)}, u32[]{:S(2)}, u32[]{:S(2)}) collective-permute-start(f32[12,768]{1,0:T(8,128)} %slice.627), channel_id=1, source_target_pairs={{0,1},{1,2},{2,3},{4,5},{5,6},{6,7},{8,9},{9,10},{10,11},{12,13},{... | collective-permute-start | bytes 110600
  520.9 21.7 %collective-permute-start.7 = (f32[12,768]{1,0:T(8,128)}, f32[12,768]{1,0:T(8,128)}, u32[]{:S(2)}, u32[]{:S(2)}) collective-permute-start(f32[12,768]{1,0:T(8,128)} %slice.632), channel_id=1, source_target_pairs={{0,1},{1,2},{2,3},{4,5},{5,6},{6,7},{8,9},{9,10},{10,11},{12,13},{... | collective-permute-start | bytes 110600
  522.8 22.7 %collective-permute-start.12 = (f32[12,768]{1,0:T(8,128)}, f32[12,768]{1,0:T(8,128)}, u32[]{:S(2)}, u32[]{:S(2)}) collective-permute-start(f32[12,768]{1,0:T(8,128)} %slice.637), channel_id=1, source_target_pairs={{0,1},{1,2},{2,3},{4,5},{5,6},{6,7},{8,9},{9,10},{10,11},{12,13},{... | collective-permute-start | bytes 110600
  525.9 22.6 %collective-permute-start.17 = (f32[12,768]{1,0:T(8,128)}, f32[12,768]{1,0:T(8,128)}, u32[]{:S(2)}, u32[]{:S(2)}) collective-permute-start(f32[12,768]{1,0:T(8,128)} %slice.642), channel_id=1, source_target_pairs={{0,1},{1,2},{2,3},{4,5},{5,6},{6,7},{8,9},{9,10},{10,11},{12,13},{... | collective-permute-start | bytes 110600
  655.3 12.1 collective-permute-start.3
  657.1 10.4 collective-permute-start.8
  660.6 7.1 collective-permute-start.13
  664.1 3.8 collective-permute-start.18
  767.6 9.6 collective-permute-start.4
  769.5 10.6 collective-permute-start.9
  771.4 11.6 collective-permute-start.14
  774.6 11.3 collective-permute-start.19
  889.8 13.0 collective-permute-start.20
  892.2 12.6 collective-permute-start.30
  897.2 14.3 collective-permute-start.25
  900.8 15.3 collective-permute-start.35
  1047.6 16.4 collective-permute-start.21
  1049.9 15.1 collective-permute-start.31
  1057.7 12.0 collective-permute-start.26
  1062.1 12.1 collective-permute-start.36
  1186.6 16.7 collective-permute-start.22
  1189.1 14.4 collective-permute-start.32
  1197.6 8.5 collective-permute-start.27
  1201.4 5.3 collective-permute-start.37
  1288.8 11.6 collective-permute-start.23
  1291.0 9.6 collective-permute-start.33
  1296.0 5.7 collective-permute-start.28
  1298.5 4.3 collective-permute-start.38
  1392.7 11.0 collective-permute-start.24
  1395.1 9.4 collective-permute-start.29
  1397.0 8.4 collective-permute-start.34
  1400.6 5.6 collective-permute-start.39
  1408.6 158.9 %reduce-scatter.120.cloned.1.call-start = ((), (), s32[]{:S(2)}) async-start(), calls=%async_computation.29 | async-start | bytes 884736
  1410.1 189.6 %reduce-scatter.104.cloned.1.call-start = ((), (), s32[]{:S(2)}) async-start(), calls=%async_computation.21 | async-start | bytes 1474560 | tf_op jit(solution)/shard_map/reduce_scatter | solution.py:484
  1413.5 216.3 %reduce-scatter.102.cloned.1.call-start = ((), (), s32[]{:S(2)}) async-start(), calls=%async_computation.20 | async-start | bytes 1474560 | tf_op jit(solution)/shard_map/reduce_scatter | solution.py:484
  1417.1 243.1 %reduce-scatter.100.cloned.1.call-start = ((), (), s32[]{:S(2)}) async-start(), calls=%async_computation.19 | async-start | bytes 1474560 | tf_op jit(solution)/shard_map/reduce_scatter | solution.py:484
  1423.5 266.9 %reduce-scatter.98.cloned.1.call-start = ((), (), s32[]{:S(2)}) async-start(), calls=%async_computation.18 | async-start | bytes 1474560 | tf_op jit(solution)/shard_map/reduce_scatter | solution.py:484
  1433.0 296.5 %reduce-scatter.122.cloned.1.call-start = ((), (), s32[]{:S(2)}) async-start(), calls=%async_computation.30 | async-start | bytes 1327104
  1438.9 332.7 %reduce-scatter.118.cloned.1.call-start = ((), (), s32[]{:S(2)}) async-start(), calls=%async_computation.28 | async-start | bytes 1769472 | tf_op jit(solution)/shard_map/reduce_scatter | solution.py:578
  1447.9 370.0 %reduce-scatter.106.cloned.1.call-start = ((), (), s32[]{:S(2)}) async-start(), calls=%async_computation.22 | async-start | bytes 2654208 | tf_op jit(solution)/shard_map/reduce_scatter | solution.py:574
  1452.3 412.3 %reduce-scatter.114.cloned.1.call-start = ((), (), s32[]{:S(2)}) async-start(), calls=%async_computation.26 | async-start | bytes 2654208 | tf_op jit(solution)/shard_map/reduce_scatter | solution.py:581
  1457.6 453.2 %reduce-scatter.116.cloned.1.call-start = ((), (), s32[]{:S(2)}) async-start(), calls=%async_computation.27 | async-start | bytes 2654208 | tf_op jit(solution)/shard_map/reduce_scatter | solution.py:582
  1463.1 494.4 %reduce-scatter.108.cloned.1.call-start = ((), (), s32[]{:S(2)}) async-start(), calls=%async_computation.23 | async-start | bytes 2654208 | tf_op jit(solution)/shard_map/reduce_scatter | solution.py:576
  1468.4 535.5 %reduce-scatter.110.cloned.1.call-start = ((), (), s32[]{:S(2)}) async-start(), calls=%async_computation.24 | async-start | bytes 2654208 | tf_op jit(solution)/shard_map/reduce_scatter | solution.py:577
  1473.8 588.3 %reduce-scatter.112.cloned.1.call-start = ((), (), s32[]{:S(2)}) async-start(), calls=%async_computation.25 | async-start | bytes 5308416 | tf_op jit(solution)/shard_map/reduce_scatter | solution.py:579
  1691.9 370.3 %copy-start.401 = (f32[5,768]{1,0:T(8,128)S(1)}, f32[5,768]{1,0:T(8,128)}, u32[]{:S(2)}) copy-start(f32[5,768]{1,0:T(8,128)} %get-tuple-element.788) | copy-start | bytes 46084
  1691.9 370.9 %copy-start.399 = (f32[10,768]{1,0:T(8,128)S(1)}, f32[10,768]{1,0:T(8,128)}, u32[]{:S(2)}) copy-start(f32[10,768]{1,0:T(8,128)} %get-tuple-element.789) | copy-start | bytes 92164
  (793 other events, 16226.6 us)
Sparse Core Ops, SparseCore 0:
  9.9 28.2 all-gather.49
  83.4 21.3 all-gather.51
  363.8 51.8 all-reduce.108
  417.6 28.3 all-gather.53
  447.9 24.0 all-gather.55
  473.9 24.1 all-gather.57
  1408.7 120.3 all-reduce.106
  1532.5 34.8 reduce-scatter.119
  1570.4 29.1 reduce-scatter.103
  1601.9 27.8 reduce-scatter.101
  1632.3 27.8 reduce-scatter.99
  1662.5 27.8 reduce-scatter.97
  1694.0 35.4 reduce-scatter.121
  1733.2 38.4 reduce-scatter.117
  1775.4 42.4 reduce-scatter.105
  1822.1 42.4 reduce-scatter.113
  1868.4 42.4 reduce-scatter.115
  1915.0 42.4 reduce-scatter.107
  1961.4 42.4 reduce-scatter.109
  2008.2 53.8 reduce-scatter.111
where the time goes:
time: 2090 us; the launch traced here: 2070 us
  blocking collectives  811 us (39%)
  waiting for transfers between devices  585 us (28%)
  local copies, waits for them, and re-layouts  234 us (11%)
  matrix products  217 us (10%)
  starting transfers between devices  103 us (5%)
  other arithmetic  92.1 us (4%)
  between operations  28.6 us (1%)
    all_gather x20, blocking collectives, unsettle(): grad_full = lax.all_gather(rounded, 'mp', axis=0, tiled=True)  277 us
    all_gather x16, blocking collectives, spread(): return lax.all_gather(share.astype(jnp.bfloat16), 'mp', axis=0, tiled=True)  219 us
    unnamed x10, blocking collectives  204 us
    unnamed x1738, local copies, waits for them, and re-layouts  123 us
    reduce_scatter x4, waiting for transfers between devices, shards(): lax.psum_scatter(image_part, 'mp', scatter_dimension=1, tiled=True)  118 us
    unnamed x43, starting transfers between devices  101 us
    unnamed x63, waiting for transfers between devices  87.5 us
    reduce_scatter x1, waiting for transfers between devices, shards(): lax.psum_scatter(merging_qkv_grad, 'dp', scatter_dimension=1, tiled=True)  58.2 us
  transfers between devices with their start and end apart: 60, of which 16 were waited for; matrix products, arithmetic and copies ran while one was open for 19% of the time, Pallas kernels for 0%

commit v1 on v0

--- a/solution.py
+++ b/solution.py
@@ -3,6 +3,8 @@
 import jax
 import jax.numpy as jnp
 from jax import lax
+from jax.experimental import pallas as pl
+from jax.experimental.pallas import tpu as pltpu
 from jax.sharding import PartitionSpec as P
 
 HEAD_DIM = 64
@@ -602,6 +604,938 @@
     )
 
 
+MESH = pl.DeviceIdType.MESH
+BF = jnp.bfloat16
+F32 = jnp.float32
+T_ATT, T_UP, T_DOWN, M_SELF, M_CROSS, M_UP, M_DOWN = range(7)
+BLOCKS = 7
+BACK_ORDER = (M_DOWN, M_UP, M_CROSS, M_SELF, T_DOWN, T_UP, T_ATT)
+SLOTS = 4
+IMAGE_PAD = 160
+NORMS = 5
+
+
+def mm(left, right):
+    return lax.dot_general(left, right, (((1,), (0,)), ((), ())), preferred_element_type=F32)
+
+
+def mm_nt(left, right):
+    return lax.dot_general(left, right, (((1,), (1,)), ((), ())), preferred_element_type=F32)
+
+
+def mm_tn(left, right):
+    return lax.dot_general(left, right, (((0,), (0,)), ((), ())), preferred_element_type=F32)
+
+
+def mm_exact(left, right, dims):
+    return lax.dot_general(
+        left, right, (dims, ((), ())), precision=EXACT_DOT_MODE, preferred_element_type=F32
+    )
+
+
+NN, NT, TN = ((1,), (0,)), ((1,), (1,)), ((0,), (0,))
+
+
+def remote(src, dst, send, recv, where):
+    return pltpu.make_async_remote_copy(
+        src_ref=src, dst_ref=dst, send_sem=send, recv_sem=recv, device_id=where, device_id_type=MESH
+    )
+
+
+def gelu_parts(pre):
+    cdf = 0.5 * (1.0 + lax.erf(pre * (1.0 / math.sqrt(2.0))))
+    return cdf
+
+
+def layers(
+    wsh, psh, bias, hid0, img, cot, tmask, cmask, id_row, id_col, gains, offs,
+    wout, mout, tgout, imout, pjout, lossout, vout,
+    G, PJ, H, XH, RSD, SQ, SK, SV, CQ, CK, CV, OA, PS, PC, PRE, ACT, XS, XR, ACC, DZ, DPRE, DQKV, DKV,
+    RC, R2, R1, RZ, BG, CT, MS, TG, IMO, IMS, IMR, IML, CG, CLS, DU, DUW, DPJ, PXS, PXR, V, VR, LS,
+    own_s, z_s, z_r, s1_s, s1_r, s2_s, s2_r, sc_s, sc_r,
+    b2_s, b2_r, b1_s, b1_r, bc_s, bc_r, bz_s, bz_r,
+    x_s, x_r, m_s, m_r, cg_s, cg_r, v_s, v_r,
+):
+    width = hid0.shape[1]
+    rows = hid0.shape[0]
+    local = width // 4
+    heads = local // HEAD_DIM
+    quarter = rows // 4
+    scale = 1.0 / math.sqrt(HEAD_DIM)
+    dp = lax.axis_index("dp")
+    z = lax.axis_index("mp")
+    y = lax.div(dp, 4)
+    x = lax.rem(lax.div(dp, 2), 2)
+    c = lax.rem(dp, 2)
+    group = lax.div(z, 2)
+    rank = lax.rem(z, 2)
+    z1 = z + 1 - 2 * rank
+    z2 = z + 2 - 4 * group
+    z3 = z1 + 2 - 4 * group
+    to_x = (dp + 2 - 4 * x, z)
+    to_y = (dp + 4 - 8 * y, z)
+    to_c = (dp + 1 - 2 * c, z)
+    to_z1, to_z2, to_z3 = (dp, z1), (dp, z2), (dp, z3)
+
+    barrier = pltpu.get_barrier_semaphore()
+    others = [(lax.rem(dp + step, 8), z) for step in range(1, 8)]
+    for where in others + [to_z1, to_z2, to_z3]:
+        pl.semaphore_signal(barrier, inc=1, device_id=where, device_id_type=MESH)
+    pl.semaphore_wait(barrier, 10)
+
+    def own(k):
+        return pltpu.make_async_copy(wsh.at[k], G.at[k, 0, y, x, c], own_s.at[k])
+
+    def hop_z(k):
+        return remote(wsh.at[k], G.at[k, 1, y, x, c], z_s.at[k], z_r.at[k], to_z2)
+
+    def hop_1(k, q):
+        if q == 0:
+            return remote(wsh.at[k], G.at[k, 0, y, x, c], s1_s.at[k, 0], s1_r.at[k, 0], to_x)
+        part = G.at[k, 1, y, x, c]
+        return remote(part, part, s1_s.at[k, 1], s1_r.at[k, 1], to_y)
+
+    def hop_2(k, q):
+        part = G.at[k, 0, y, :, c] if q == 0 else G.at[k, 1, :, x, c]
+        return remote(part, part, s2_s.at[k, q], s2_r.at[k, q], to_y if q == 0 else to_x)
+
+    def hop_c(k, q):
+        part = G.at[k, q, :, :, c]
+        return remote(part, part, sc_s.at[k, q], sc_r.at[k, q], to_c)
+
+    p_own = pltpu.make_async_copy(psh, PJ.at[y, x, c], own_s.at[BLOCKS])
+    p_1 = remote(psh, PJ.at[y, x, c], s1_s.at[BLOCKS, 0], s1_r.at[BLOCKS, 0], to_x)
+    p_2 = remote(PJ.at[y, :, c], PJ.at[y, :, c], s2_s.at[BLOCKS, 0], s2_r.at[BLOCKS, 0], to_y)
+    p_c = remote(PJ.at[:, :, c], PJ.at[:, :, c], sc_s.at[BLOCKS, 0], sc_r.at[BLOCKS, 0], to_c)
+
+    def tick(j):
+        k = j
+        if k < BLOCKS:
+            own(k).start()
+            hop_z(k).start()
+            hop_1(k, 0).start()
+        elif k == BLOCKS:
+            p_own.start()
+            p_1.start()
+        k = j - 1
+        if 0 <= k < BLOCKS:
+            hop_z(k).wait_recv()
+            hop_1(k, 1).start()
+        k = j - 2
+        if 0 <= k < BLOCKS:
+            own(k).wait()
+            for q in range(2):
+                hop_1(k, q).wait_recv()
+                hop_2(k, q).start()
+        elif k == BLOCKS:
+            p_own.wait()
+            p_1.wait_recv()
+            p_2.start()
+        k = j - 3
+        if 0 <= k < BLOCKS:
+            for q in range(2):
+                hop_2(k, q).wait_recv()
+                hop_c(k, q).start()
+        elif k == BLOCKS:
+            p_2.wait_recv()
+            p_c.start()
+        k = j - 4
+        if 0 <= k < BLOCKS:
+            for q in range(2):
+                hop_c(k, q).wait_recv()
+        elif k == BLOCKS:
+            p_c.wait_recv()
+
+    def sent_all():
+        for k in range(BLOCKS):
+            hop_z(k).wait_send()
+            for q in range(2):
+                hop_1(k, q).wait_send()
+                hop_2(k, q).wait_send()
+                hop_c(k, q).wait_send()
+        p_1.wait_send()
+        p_2.wait_send()
+        p_c.wait_send()
+
+    def swap(e):
+        return remote(XS.at[e % 2], XR.at[e], x_s.at[e % 2], x_r.at[e], to_z1)
+
+    def swap_start(e):
+        if e >= 2:
+            swap(e - 2).wait_send()
+        XS[e % 2] = ACC[...].astype(BF)
+        swap(e).start()
+
+    def swap_sum(e):
+        swap(e).wait_recv()
+        return XS[e % 2].astype(F32) + XR[e].astype(F32)
+
+    bias_copy = remote(bias, BG.at[1], m_s.at[0], m_r.at[0], to_z2)
+    bias_copy.start()
+    BG[0] = bias[...]
+    cot_copies = [
+        remote(cot.at[group], CT.at[z], m_s.at[1], m_r.at[1], to_z1),
+        remote(cot.at[1 - group], CT.at[z], m_s.at[2], m_r.at[2], to_z2),
+        remote(cot.at[1 - group], CT.at[z], m_s.at[3], m_r.at[3], to_z3),
+    ]
+
+    for j in range(4):
+        tick(j)
+    bias_copy.wait()
+    for copy in cot_copies:
+        copy.start()
+    CT[z] = cot[group]
+
+    def weight(k, q, lo, hi):
+        return G[k, q, :, :, :, :, lo:hi].reshape(width, hi - lo)
+
+    def norm_forward(e, before):
+        centre = before - jnp.mean(before, -1, keepdims=True)
+        inverse = lax.rsqrt(jnp.mean(centre * centre, -1, keepdims=True) + EPS)
+        xhat = centre * inverse
+        XH[e] = xhat
+        RSD[e] = inverse
+        return xhat * gains[e : e + 1, :] + offs[NORMS + e : NORMS + e + 1, :]
+
+    def settle_forward(e):
+        before = H[e].astype(F32) + offs[e : e + 1, :] + swap_sum(e)
+        out = norm_forward(e, before)
+        if e + 1 < NORMS:
+            H[e + 1] = out.astype(BF)
+        return out
+
+    def softmax(scores, mask):
+        scores = jnp.where(mask > 0, scores * scale, NEGATIVE)
+        raised = jnp.exp(scores - jnp.max(scores, -1, keepdims=True))
+        return raised / jnp.sum(raised, -1, keepdims=True)
+
+    def self_attention(k, e, layer):
+        ACC[...] = jnp.zeros_like(ACC)
+
+        def part(q, carry):
+            made = mm(H[e], weight(k, q, 0, 3 * local))
+            queries = (made[:, :local] + BG[q, 2 * layer : 2 * layer + 1, :local]).astype(BF)
+            keys = made[:, local : 2 * local].astype(BF)
+            values = (
+                made[:, 2 * local :] + BG[q, 2 * layer + 1 : 2 * layer + 2, :local]
+            ).astype(BF)
+            SQ[layer, q], SK[layer, q], SV[layer, q] = queries, keys, values
+            mixed = []
+            for n in range(heads):
+                cut = slice(n * HEAD_DIM, (n + 1) * HEAD_DIM)
+                probs = softmax(mm_nt(queries[:, cut], keys[:, cut]), tmask[...]).astype(BF)
+                PS[layer, q, n] = probs
+                mixed.append(mm(probs, values[:, cut]).astype(BF))
+            mixed = jnp.concatenate(mixed, 1)
+            OA[layer, q] = mixed
+            ACC[...] += mm_nt(mixed, weight(k, q, 3 * local, 4 * local))
+            return carry
+
+        lax.fori_loop(0, 2, part, 0)
+
+    def image_keys():
+        def part(q, carry):
+            made = mm(img[...], weight(M_CROSS, q, local, 3 * local))
+            CK[q] = made[:, :local].astype(BF)
+            CV[q] = (made[:, local:] + BG[q, 5:6, :local]).astype(BF)
+            return carry
+
+        lax.fori_loop(0, 2, part, 0)
+
+    def cross_attention():
+        ACC[...] = jnp.zeros_like(ACC)
+
+        def part(q, carry):
+            queries = (mm(H[3], weight(M_CROSS, q, 0, local)) + BG[q, 4:5, :local]).astype(BF)
+            CQ[q] = queries
+            mixed = []
+            for n in range(heads):
+                cut = slice(n * HEAD_DIM, (n + 1) * HEAD_DIM)
+                probs = softmax(mm_nt(queries[:, cut], CK[q, :, cut]), cmask[...]).astype(BF)
+                PC[q, n] = probs
+                mixed.append(mm(probs, CV[q, :, cut]).astype(BF))
+            mixed = jnp.concatenate(mixed, 1)
+            OA[2, q] = mixed
+            ACC[...] += mm_nt(mixed, weight(M_CROSS, q, 3 * local, 4 * local))
+            return carry
+
+        lax.fori_loop(0, 2, part, 0)
+
+    def feed_up(k, e, layer):
+        def part(q, carry):
+            pre = mm(H[e], weight(k, q, 0, width)) + BG[q, 6 + layer : 7 + layer, :]
+            PRE[layer, q] = pre
+            ACT[layer, q] = (pre * gelu_parts(pre)).astype(BF)
+            return carry
+
+        lax.fori_loop(0, 2, part, 0)
+
+    def feed_down(k, layer):
+        ACC[...] = jnp.zeros_like(ACC)
+
+        def part(q, carry):
+            ACC[...] += mm_nt(ACT[layer, q], weight(k, q, 0, width))
+            return carry
+
+        lax.fori_loop(0, 2, part, 0)
+
+    H[0] = hid0[...]
+    tick(4)
+    self_attention(T_ATT, 0, 0)
+    swap_start(0)
+    tick(5)
+    settle_forward(0)
+    feed_up(T_UP, 1, 0)
+    tick(6)
+    feed_down(T_DOWN, 0)
+    swap_start(1)
+    tick(7)
+    settle_forward(1)
+
+    def summary_rows():
+        spot = lax.broadcasted_iota(jnp.int32, (8, rows), 0)
+        place = lax.broadcasted_iota(jnp.int32, (8, rows), 1)
+        pick = jnp.where((place == spot * (quarter // 4)) & (spot < 4), 1.0, 0.0).astype(BF)
+        text_rows = mm(pick, H[2])
+        spot = lax.broadcasted_iota(jnp.int32, (8, img.shape[0]), 0)
+        place = lax.broadcasted_iota(jnp.int32, (8, img.shape[0]), 1)
+        pick = jnp.where((place == spot * IMAGE_PAD) & (spot < 4), 1.0, 0.0).astype(BF)
+        image_rows = mm(pick, img[...])
+        CLS[...] = jnp.concatenate([text_rows, image_rows], 0).astype(BF)
+        CG[dp] = CLS[...]
+
+    summary_rows()
+    summary = [
+        remote(CLS, CG.at[dp], cg_s.at[i], cg_r.at[i], where) for i, where in enumerate(others)
+    ]
+    self_attention(M_SELF, 2, 1)
+    swap_start(2)
+    for copy in summary:
+        copy.start()
+    tick(8)
+    image_keys()
+    settle_forward(2)
+    cross_attention()
+    swap_start(3)
+    tick(9)
+    settle_forward(3)
+    feed_up(M_UP, 4, 1)
+    tick(10)
+    feed_down(M_DOWN, 1)
+    swap_start(4)
+    tick(11)
+    merged = settle_forward(4)
+    MS[...] = merged.reshape(4, quarter, width)
+    mout[group] = MS[z]
+    merged_copy = remote(MS.at[z2], mout.at[group], m_s.at[4], m_r.at[4], to_z2)
+    merged_copy.start()
+    sent_all()
+
+    def back_c(k, q):
+        slot = BACK_ORDER.index(k) % SLOTS
+        return remote(
+            G.at[k, q, :, :, 1 - c], RC.at[slot, q], bc_s.at[k, q], bc_r.at[k, q], to_c
+        )
+
+    def back_2(k, q):
+        part = G.at[k, 0, 1 - y, :, c] if q == 0 else G.at[k, 1, :, 1 - x, c]
+        return remote(part, R2.at[k, q], b2_s.at[k, q], b2_r.at[k, q], to_y if q == 0 else to_x)
+
+    def back_1(k, q):
+        part = G.at[k, 0, y, 1 - x, c] if q == 0 else G.at[k, 1, 1 - y, x, c]
+        return remote(part, R1.at[k, q], b1_s.at[k, q], b1_r.at[k, q], to_x if q == 0 else to_y)
+
+    def back_z(k):
+        return remote(G.at[k, 1, y, x, c], RZ.at[k], bz_s.at[k], bz_r.at[k], to_z2)
+
+    def both(a, b):
+        return (a.astype(F32) + b.astype(F32)).astype(BF)
+
+    def back_tick(j):
+        n = j
+        if n < BLOCKS:
+            for q in range(2):
+                back_c(BACK_ORDER[n], q).start()
+        n = j - 1
+        if 0 <= n < BLOCKS:
+            k = BACK_ORDER[n]
+            for q in range(2):
+                back_c(k, q).wait()
+                for a in range(2):
+                    for b in range(2):
+                        G[k, q, a, b, c] = both(G[k, q, a, b, c], RC[n % SLOTS, q, a, b])
+                back_2(k, q).start()
+        n = j - 2
+        if 0 <= n < BLOCKS:
+            k = BACK_ORDER[n]
+            for q in range(2):
+                back_2(k, q).wait()
+                for a in range(2):
+                    if q == 0:
+                        G[k, 0, y, a, c] = both(G[k, 0, y, a, c], R2[k, 0, a])
+                    else:
+                        G[k, 1, a, x, c] = both(G[k, 1, a, x, c], R2[k, 1, a])
+                back_1(k, q).start()
+        n = j - 3
+        if 0 <= n < BLOCKS:
+            k = BACK_ORDER[n]
+            back_1(k, 1).wait()
+            G[k, 1, y, x, c] = both(G[k, 1, y, x, c], R1[k, 1])
+            back_z(k).start()
+            back_1(k, 0).wait()
+            wout[k] = G[k, 0, y, x, c].astype(F32) + R1[k, 0].astype(F32)
+        n = j - 4
+        if 0 <= n < BLOCKS:
+            k = BACK_ORDER[n]
+            back_z(k).wait()
+            wout[k] = wout[k] + RZ[k].astype(F32)
+
+    V[...] = jnp.zeros_like(V)
+
+    def norm_backward(e, grad):
+        xhat = XH[e]
+        V[e : e + 1, :] = jnp.sum(grad * xhat, 0, keepdims=True)
+        V[2 * NORMS + e : 2 * NORMS + e + 1, :] = jnp.sum(grad, 0, keepdims=True)
+        scaled = grad * gains[e : e + 1, :]
+        first = jnp.mean(scaled, -1, keepdims=True)
+        second = jnp.mean(scaled * xhat, -1, keepdims=True)
+        grad = RSD[e] * (scaled - first - xhat * second)
+        DZ[...] = grad
+        rounded = grad.astype(BF)
+        V[NORMS + e : NORMS + e + 1, :] = jnp.sum(rounded.astype(F32), 0, keepdims=True)
+        return rounded
+
+    def keep_grad(k, q, lo, value):
+        value = value.astype(BF)
+        G[k, q, :, :, :, :, lo : lo + value.shape[1]] = value.reshape(
+            2, 2, 2, width // 8, value.shape[1]
+        )
+
+    def feed_backward(up, down, e, layer, rounded):
+        ACC[...] = jnp.zeros_like(ACC)
+
+        def part(q, carry):
+            grad = mm(rounded, weight(down, q, 0, width))
+            pre = PRE[layer, q]
+            slope = gelu_parts(pre) + pre * (
+                jnp.exp(-0.5 * pre * pre) * (1.0 / math.sqrt(2.0 * math.pi))
+            )
+            grad = (grad * slope).astype(BF)
+            DPRE[q] = grad
+            V[pl.ds(15 + 2 * q + layer, 1), :] = jnp.sum(grad.astype(F32), 0, keepdims=True)
+            ACC[...] += mm_nt(grad, weight(up, q, 0, width))
+            return carry
+
+        lax.fori_loop(0, 2, part, 0)
+
+    def feed_down_grad(down, layer, rounded):
+        turned = rounded.T
+
+        def part(q, carry):
+            keep_grad(down, q, 0, mm(turned, ACT[layer, q]))
+            return carry
+
+        lax.fori_loop(0, 2, part, 0)
+
+    def feed_up_grad(up, e):
+        turned = H[e].T
+
+        def part(q, carry):
+            keep_grad(up, q, 0, mm(turned, DPRE[q]))
+            return carry
+
+        lax.fori_loop(0, 2, part, 0)
+
+    def head_backward(probs, queries, keys, values, grad):
+        wide = probs.astype(F32)
+        grad_values = mm_tn(probs, grad)
+        grad_probs = mm_nt(grad, values)
+        grad_scores = wide * (grad_probs - jnp.sum(grad_probs * wide, -1, keepdims=True))
+        grad_scores = grad_scores.astype(BF)
+        grad_queries = mm(grad_scores, keys) * scale
+        grad_keys = mm_tn(grad_scores, queries) * scale
+        return grad_queries.astype(BF), grad_keys.astype(BF), grad_values.astype(BF)
+
+    def bias_sums(q, layer, grad_queries, grad_values):
+        V[pl.ds(19 + 6 * q + 2 * layer, 1), 0:local] = jnp.sum(
+            grad_queries.astype(F32), 0, keepdims=True
+        )
+        V[pl.ds(20 + 6 * q + 2 * layer, 1), 0:local] = jnp.sum(
+            grad_values.astype(F32), 0, keepdims=True
+        )
+
+    def self_backward(k, layer, rounded):
+        ACC[...] = jnp.zeros_like(ACC)
+
+        def part(q, carry):
+            grad_mixed = mm(rounded, weight(k, q, 3 * local, 4 * local)).astype(BF)
+            parts = []
+            for n in range(heads):
+                cut = slice(n * HEAD_DIM, (n + 1) * HEAD_DIM)
+                parts.append(
+                    head_backward(
+                        PS[layer, q, n],
+                        SQ[layer, q, :, cut],
+                        SK[layer, q, :, cut],
+                        SV[layer, q, :, cut],
+                        grad_mixed[:, cut],
+                    )
+                )
+            made = [jnp.concatenate([part[i] for part in parts], 1) for i in range(3)]
+            bias_sums(q, layer, made[0], made[2])
+            grads = jnp.concatenate(made, 1)
+            DQKV[q] = grads
+            ACC[...] += mm_nt(grads, weight(k, q, 0, 3 * local))
+            return carry
+
+        lax.fori_loop(0, 2, part, 0)
+
+    def self_grad(k, e, layer, rounded):
+        turned = H[e].T
+        turned_out = rounded.T
+
+        def part(q, carry):
+            keep_grad(
+                k,
+                q,
+                0,
+                jnp.concatenate(
+                    [mm(turned, DQKV[q]), mm(turned_out, OA[layer, q])], 1
+                ),
+            )
+            return carry
+
+        lax.fori_loop(0, 2, part, 0)
+
+    def cross_backward(rounded):
+        ACC[...] = jnp.zeros_like(ACC)
+
+        def part(q, carry):
+            grad_mixed = mm(rounded, weight(M_CROSS, q, 3 * local, 4 * local)).astype(BF)
+            parts = []
+            for n in range(heads):
+                cut = slice(n * HEAD_DIM, (n + 1) * HEAD_DIM)
+                parts.append(
+                    head_backward(
+                        PC[q, n],
+                        CQ[q, :, cut],
+                        CK[q, :, cut],
+                        CV[q, :, cut],
+                        grad_mixed[:, cut],
+                    )
+                )
+            made = [jnp.concatenate([part[i] for part in parts], 1) for i in range(3)]
+            bias_sums(q, 2, made[0], made[2])
+            DQKV[q, :, 0:local] = made[0]
+            DKV[q] = jnp.concatenate(made[1:], 1)
+            ACC[...] += mm_nt(made[0], weight(M_CROSS, q, 0, local))
+            return carry
+
+        lax.fori_loop(0, 2, part, 0)
+
+    def image_columns(first, second):
+        def rows_of(q, place):
+            part = G[M_CROSS, q, lax.div(place, 2), lax.rem(place, 2), :, :, local : 3 * local]
+            return part.reshape(local, 2 * local)
+
+        total = None
+        for q in range(2):
+            turned = jnp.concatenate([rows_of(q, first), rows_of(q, second)], 0)
+            term = mm_nt(DKV[q], turned)
+            total = term if total is None else total + term
+        return total
+
+    def cross_grad(rounded):
+        turned = H[3].T
+        turned_out = rounded.T
+        turned_image = img[...].T
+
+        def part(q, carry):
+            keep_grad(
+                M_CROSS,
+                q,
+                0,
+                jnp.concatenate(
+                    [
+                        mm(turned, DQKV[q, :, 0:local]),
+                        mm(turned_image, DKV[q]),
+                        mm(turned_out, OA[2, q]),
+                    ],
+                    1,
+                ),
+            )
+            return carry
+
+        lax.fori_loop(0, 2, part, 0)
+
+    def contrast():
+        spots = CG.shape[0] * 8
+        proj = PJ[...].reshape(width, PJ.shape[-1])
+        half = proj.shape[1] // 2
+        text_rows = CG[:, 0:8, :].reshape(spots, width)
+        image_rows = CG[:, 8:16, :].reshape(spots, width)
+        raw_t = mm(text_rows, proj[:, :half])
+        raw_w = mm(image_rows, proj[:, half:])
+        inv_t = lax.rsqrt(jnp.sum(raw_t * raw_t, -1, keepdims=True) + EPS)
+        inv_w = lax.rsqrt(jnp.sum(raw_w * raw_w, -1, keepdims=True) + EPS)
+        t, w = raw_t * inv_t, raw_w * inv_w
+        row_key, col_key = id_row[:, 0:1], id_col[0:1, 0:spots]
+        row_batch, col_batch = id_row[:, 1:2], id_col[1:2, 0:spots]
+        live = row_batch == col_batch
+        same = jnp.where(live & (row_key == col_key), 1.0, 0.0)
+        target = same / jnp.sum(same, 1, keepdims=True)
+
+        def log_rows(scores):
+            scores = jnp.where(live, scores / SCORE_SCALE, NEGATIVE)
+            shifted = scores - jnp.max(scores, -1, keepdims=True)
+            return shifted - jnp.log(jnp.sum(jnp.exp(shifted), -1, keepdims=True))
+
+        log_t = log_rows(mm_exact(t, w, NT))
+        log_w = log_rows(mm_exact(w, t, NT))
+        loss = -0.5 * (
+            jnp.sum(target * jnp.where(live, log_t, 0.0), 1, keepdims=True)
+            + jnp.sum(target * jnp.where(live, log_w, 0.0), 1, keepdims=True)
+        )
+        over_t = (0.5 / SCORE_SCALE) * (jnp.exp(log_t) - target)
+        over_w = (0.5 / SCORE_SCALE) * (jnp.exp(log_w) - target)
+        grad_t = mm_exact(over_t, w, NN) + mm_exact(over_w, w, TN)
+        grad_w = mm_exact(over_t, t, TN) + mm_exact(over_w, t, NN)
+        grad_t = (grad_t - t * jnp.sum(t * grad_t, -1, keepdims=True)) * inv_t
+        grad_w = (grad_w - w * jnp.sum(w * grad_w, -1, keepdims=True)) * inv_w
+        valid = id_row[:, 2:3]
+        grad_t, grad_w = grad_t * valid, grad_w * valid
+        DU[...] = grad_t.reshape(8, 8, half)
+        DUW[...] = grad_w.reshape(8, 8, half)
+        LS[...] = jnp.broadcast_to(loss, (spots, 128)).reshape(8, 8, 128)
+        DPJ[:, :, 0:half] = mm_exact(text_rows.astype(F32), grad_t, TN).reshape(
+            8, width // 8, half
+        )
+        DPJ[:, :, half:] = mm_exact(image_rows.astype(F32), grad_w, TN).reshape(
+            8, width // 8, half
+        )
+        PXS[0 : width // 8, :] = DPJ[dp]
+        PXS[width // 8 :, :] = jnp.concatenate([LS[dp]] * (PXS.shape[1] // 128), 1)
+
+    pair_copy = remote(PXS, PXR, m_s.at[5], m_r.at[5], to_z2)
+
+    for copy in cot_copies:
+        copy.wait()
+    grad = jnp.concatenate([CT[i].astype(F32)[:quarter] for i in range(4)], 0)
+    rounded = norm_backward(4, grad)
+    feed_backward(M_UP, M_DOWN, 4, 1, rounded)
+    swap_start(5)
+    feed_down_grad(M_DOWN, 1, rounded)
+    back_tick(0)
+    feed_up_grad(M_UP, 4)
+    back_tick(1)
+    rounded = norm_backward(3, DZ[...] + swap_sum(5))
+    cross_backward(rounded)
+    swap_start(6)
+    IMS[...] = image_columns(z1, z3).astype(BF)
+    image_copy = remote(IMS, IMR, m_s.at[6], m_r.at[6], to_z1)
+    image_copy.start()
+    IMO[...] = image_columns(z, z2)
+    cross_grad(rounded)
+    back_tick(2)
+    rounded = norm_backward(2, DZ[...] + swap_sum(6))
+    self_backward(M_SELF, 1, rounded)
+    swap_start(7)
+    self_grad(M_SELF, 2, 1, rounded)
+    back_tick(3)
+    for copy in summary:
+        copy.wait()
+    contrast()
+    pair_copy.start()
+
+    proj_text = PJ[:, :, :, :, 0 : PJ.shape[-1] // 2].reshape(width, PJ.shape[-1] // 2)
+    extra = mm_exact(DU[dp], proj_text.astype(F32), NT)
+    place = lax.broadcasted_iota(jnp.int32, (rows, width), 0)
+    grad = DZ[...] + swap_sum(7)
+    for n in range(4):
+        grad = grad + jnp.where(place == n * (quarter // 4), extra[n : n + 1, :], 0.0)
+    rounded = norm_backward(1, grad)
+    feed_backward(T_UP, T_DOWN, 1, 0, rounded)
+    swap_start(8)
+    feed_down_grad(T_DOWN, 0, rounded)
+    back_tick(4)
+    feed_up_grad(T_UP, 1)
+    back_tick(5)
+    rounded = norm_backward(0, DZ[...] + swap_sum(8))
+    self_backward(T_ATT, 0, rounded)
+    swap_start(9)
+    self_grad(T_ATT, 0, 0, rounded)
+    back_tick(6)
+
+    stat_to = (to_c, to_x, to_y, to_z2)
+
+    def stat_copy(i):
+        return remote(V, VR.at[i], v_s.at[i], v_r.at[i], stat_to[i])
+
+    stat_copy(0).start()
+
+    def image_extra(place):
+        part = PJ[lax.div(place, 2), lax.rem(place, 2), :, :, PJ.shape[-1] // 2 :]
+        return mm_exact(DUW[dp], part.reshape(local, PJ.shape[-1] // 2).astype(F32), NT)
+
+    image_copy.wait()
+    IMO[...] += IMR[...].astype(F32)
+    extra = jnp.concatenate([image_extra(z), image_extra(z2)], 1)
+    first_row = lax.broadcasted_iota(jnp.int32, (8, 2 * local), 0) == 0
+    for n in range(4):
+        span = slice(n * IMAGE_PAD, n * IMAGE_PAD + 8)
+        IMO[span, :] = IMO[span, :] + jnp.where(first_row, extra[n : n + 1, :], 0.0)
+    imout[group] = IMO[:, :local].astype(BF)
+    IML[...] = IMO[:, local:].astype(BF)
+    image_last = remote(IML, imout.at[group], m_s.at[7], m_r.at[7], to_z2)
+    image_last.start()
+
+    grad = DZ[...] + swap_sum(9)
+    TG[...] = grad.reshape(4, quarter, width)
+    tgout[group] = TG[z]
+    text_copy = remote(TG.at[z2], tgout.at[group], m_s.at[8], m_r.at[8], to_z2)
+    text_copy.start()
+    for i in range(4):
+        back_tick(7 + i)
+        stat_copy(i).wait()
+        if i < 3:
+            V[...] = V[...] + VR[i]
+            stat_copy(i + 1).start()
+    vout[0:15, :] = V[0:15, :] + VR[3, 0:15, :]
+    vout[16:18, :] = V[15:17, :] + VR[3, 17:19, :]
+    vout[24:30, :] = V[19:25, :] + VR[3, 25:31, :]
+    pair_copy.wait()
+    pjout[...] = PXS[0 : width // 8, :] + PXR[0 : width // 8, :]
+    lossout[group] = PXS[width // 8 :, 0:128]
+    lossout[1 - group] = PXR[width // 8 :, 0:128]
+    image_last.wait()
+    text_copy.wait()
+    merged_copy.wait()
+    swap(8).wait_send()
+    swap(9).wait_send()
+
+
+def fast_shards(
+    text_embeds,
+    text_lengths,
+    image_embeds,
+    image_mask,
+    image_ids,
+    out_cot,
+    text_qkv,
+    text_out,
+    text_up,
+    text_down,
+    merge_qkv,
+    merge_out,
+    merge_up,
+    merge_down,
+    projections,
+    norm_gains,
+    offsets,
+    head_biases,
+    up_biases,
+):
+    micro, pairs, tokens, width = text_embeds.shape
+    images = image_embeds.shape[2]
+    data_parts = lax.axis_size("dp")
+    model_parts = lax.axis_size("mp")
+    z = lax.axis_index("mp")
+    group = z // 2
+    local = width // model_parts
+    shard = width // data_parts
+    half_micro = micro // 2
+    groups = 2
+    count = half_micro * pairs
+    share = tokens // model_parts
+    rows = count * tokens
+    quarter = rows // model_parts
+
+    def mine(array):
+        return lax.dynamic_slice_in_dim(array, group * half_micro, half_micro, 0)
+
+    def attention_block(qkv, out):
+        return jnp.concatenate([qkv[0], qkv[1], qkv[2], out.T], 1)
+
+    wsh = jnp.stack(
+        [
+            attention_block(text_qkv, text_out),
+            text_up,
+            text_down.T,
+            attention_block(merge_qkv[:3], merge_out[0]),
+            attention_block(merge_qkv[3:], merge_out[1]),
+            merge_up,
+            merge_down.T,
+        ]
+    )
+    psh = jnp.concatenate([projections[0], projections[1]], 1)
+    bias = jnp.concatenate(
+        [jnp.pad(head_biases, ((0, 0), (0, width - local))), up_biases], 0
+    )
+    hid0 = (
+        mine(text_embeds)
+        .reshape(half_micro, pairs, model_parts, share, width)
+        .transpose(2, 0, 1, 3, 4)
+        .reshape(rows, width)
+    )
+    img = jnp.pad(
+        mine(image_embeds), ((0, 0), (0, 0), (0, IMAGE_PAD - images), (0, 0))
+    ).reshape(count * IMAGE_PAD, width)
+    cot = jnp.pad(
+        out_cot.reshape(groups, quarter, width), ((0, 0), (0, 48 - quarter), (0, 0))
+    )
+    lengths = mine(text_lengths).reshape(count)
+    place = jnp.arange(rows)
+    pair_of = (place // share) % count
+    token_of = (place // quarter) * share + place % share
+    text_live = token_of < lengths[pair_of]
+    tmask = ((pair_of[:, None] == pair_of[None, :]) & text_live[None, :]).astype(jnp.float32)
+    image_live = jnp.pad(
+        mine(image_mask), ((0, 0), (0, 0), (0, IMAGE_PAD - images))
+    ).reshape(count * IMAGE_PAD)
+    image_of = jnp.arange(count * IMAGE_PAD) // IMAGE_PAD
+    cmask = ((pair_of[:, None] == image_of[None, :]) & (image_live > 0)[None, :]).astype(
+        jnp.float32
+    )
+    ids = mine(image_ids).reshape(half_micro, data_parts, pairs).transpose(1, 0, 2)
+    batch = jnp.broadcast_to(jnp.arange(half_micro)[None, :, None], ids.shape)
+    live = jnp.ones_like(ids)
+
+    def spots(array, fill):
+        array = array.reshape(data_parts, count)
+        return jnp.pad(
+            array, ((0, 0), (0, 8 - count)), constant_values=fill
+        ).reshape(data_parts * 8)
+
+    table = jnp.stack([spots(ids, 0), spots(batch, -1), spots(live, 0)]).astype(jnp.float32)
+    id_row = jnp.pad(table.T, ((0, 0), (0, 125)))
+    id_col = jnp.pad(table, ((0, 5), (0, 128 - data_parts * 8)))
+
+    vmem = pl.BlockSpec(memory_space=pltpu.VMEM)
+
+    def sem(*shape):
+        return pltpu.SemaphoreType.DMA(shape)
+
+    def buf(*shape, dtype=BF):
+        return pltpu.VMEM(shape, dtype)
+
+    grid = (2, 2, 2, shard)
+    scratch = [
+        buf(BLOCKS, 2, *grid, width),
+        buf(*grid, psh.shape[1]),
+        buf(NORMS, rows, width),
+        buf(NORMS, rows, width, dtype=F32),
+        buf(NORMS, rows, 1, dtype=F32),
+        buf(2, 2, rows, local),
+        buf(2, 2, rows, local),
+        buf(2, 2, rows, local),
+        buf(2, rows, local),
+        buf(2, count * IMAGE_PAD, local),
+        buf(2, count * IMAGE_PAD, local),
+        buf(3, 2, rows, local),
+        buf(2, 2, local // HEAD_DIM, rows, rows),
+        buf(2, local // HEAD_DIM, rows, count * IMAGE_PAD),
+        buf(2, 2, rows, width, dtype=F32),
+        buf(2, 2, rows, width),
+        buf(2, rows, width),
+        buf(2 * NORMS, rows, width),
+        buf(rows, width, dtype=F32),
+        buf(rows, width, dtype=F32),
+        buf(2, rows, width),
+        buf(2, rows, 3 * local),
+        buf(2, count * IMAGE_PAD, 2 * local),
+        buf(SLOTS, 2, 2, 2, shard, width),
+        buf(BLOCKS, 2, 2, shard, width),
+        buf(BLOCKS, 2, shard, width),
+        buf(BLOCKS, shard, width),
+        buf(2, 8, width, dtype=F32),
+        buf(model_parts, 48, width),
+        buf(model_parts, quarter, width, dtype=F32),
+        buf(model_parts, quarter, width, dtype=F32),
+        buf(count * IMAGE_PAD, 2 * local, dtype=F32),
+        buf(count * IMAGE_PAD, 2 * local),
+        buf(count * IMAGE_PAD, 2 * local),
+        buf(count * IMAGE_PAD, local),
+        buf(data_parts, 16, width),
+        buf(16, width),
+        buf(data_parts, 8, psh.shape[1] // 2, dtype=F32),
+        buf(data_parts, 8, psh.shape[1] // 2, dtype=F32),
+        buf(data_parts, shard, psh.shape[1], dtype=F32),
+        buf(shard + 8, psh.shape[1], dtype=F32),
+        buf(shard + 8, psh.shape[1], dtype=F32),
+        buf(32, width, dtype=F32),
+        buf(4, 32, width, dtype=F32),
+        buf(data_parts, 8, 128, dtype=F32),
+        sem(BLOCKS + 1),
+        sem(BLOCKS),
+        sem(BLOCKS),
+        *[sem(BLOCKS + 1, 2) for _ in range(6)],
+        *[sem(BLOCKS, 2) for _ in range(6)],
+        *[sem(BLOCKS) for _ in range(2)],
+        sem(2),
+        sem(2 * NORMS),
+        sem(9),
+        sem(9),
+        sem(data_parts - 1),
+        sem(data_parts - 1),
+        sem(4),
+        sem(4),
+    ]
+    inputs = (
+        wsh, psh, bias, hid0, img, cot, tmask, cmask, id_row, id_col, norm_gains, offsets,
+    )
+    wout, mout, tgout, imout, pjout, lossout, vout = pl.pallas_call(
+        layers,
+        out_shape=(
+            jax.ShapeDtypeStruct((BLOCKS, shard, width), F32),
+            jax.ShapeDtypeStruct((groups, quarter, width), F32),
+            jax.ShapeDtypeStruct((groups, quarter, width), F32),
+            jax.ShapeDtypeStruct((groups, count * IMAGE_PAD, local), BF),
+            jax.ShapeDtypeStruct((shard, psh.shape[1]), F32),
+            jax.ShapeDtypeStruct((groups, 8, 128), F32),
+            jax.ShapeDtypeStruct((32, width), F32),
+        ),
+        in_specs=[vmem] * len(inputs),
+        out_specs=(vmem,) * 7,
+        scratch_shapes=scratch,
+        compiler_params=pltpu.CompilerParams(
+            collective_id=0, has_side_effects=True, vmem_limit_bytes=63 * 2**20
+        ),
+    )(*inputs)
+
+    def parts(block, number):
+        return block.reshape(shard, number, local).transpose(1, 0, 2)
+
+    def text_shape(array):
+        return array.reshape(micro, pairs, share, width)
+
+    split = 3 * local
+    image_grad = (
+        imout.reshape(micro, pairs, IMAGE_PAD, local)[:, :, :images].astype(F32)
+    )
+    loss = lossout[:, :count, 0].reshape(micro, pairs)
+    return (
+        text_shape(mout),
+        loss,
+        text_shape(tgout),
+        image_grad,
+        parts(wout[T_ATT, :, :split], 3),
+        wout[T_ATT, :, split:].T,
+        wout[T_UP],
+        wout[T_DOWN].T,
+        jnp.concatenate(
+            [parts(wout[M_SELF, :, :split], 3), parts(wout[M_CROSS, :, :split], 3)], 0
+        ),
+        jnp.stack([wout[M_SELF, :, split:].T, wout[M_CROSS, :, split:].T]),
+        wout[M_UP],
+        wout[M_DOWN].T,
+        pjout.reshape(shard, 2, -1).transpose(1, 0, 2),
+        vout[0:5],
+        vout[5:15],
+        vout[24:30, :local],
+        vout[16:18],
+    )
+
+
 def solution(mesh):
     placed = (
         P(None, "dp", None, None),
@@ -624,8 +1558,9 @@
         P(None, "mp"),
         P(None, "mp"),
     )
+    small = mesh.shape["dp"] == 8 and mesh.shape["mp"] == 4
     return jax.shard_map(
-        shards,
+        fast_shards if small else shards,
         mesh=mesh,
         in_specs=placed,
         out_specs=(

time: 2090 us -> 271 us (0.13)
  blocking collectives: 811 us -> 0 us
  waiting for transfers between devices: 585 us -> 0 us
  Pallas kernels: 0 us -> 223 us
  matrix products: 217 us -> 0 us
  local copies, waits for them, and re-layouts: 234 us -> 35 us
  starting transfers between devices: 103 us -> 0 us
  other arithmetic: 92.1 us -> 10.8 us
  between operations: 28.6 us -> 0.94 us
    all_gather x48 -> x0, blocking collectives: 607 us -> none  [the longest x20 277 us: unsettle(): grad_full = lax.all_gather(rounded, 'mp', axis=0, tiled=True)]
    reduce_scatter x11 -> x0, waiting for transfers between devices: 449 us -> none  [the longest x4 118 us: shards(): lax.psum_scatter(image_part, 'mp', scatter_dimension=1, tiled=True)]
    pallas_call x0 -> x1, Pallas kernels: none -> 223 us  [fast_shards(): pl.pallas_call(layers, out_shape=(jax.ShapeDtypeStruct((BLOCKS, shard, wi...]
    dot_general x252 -> x0, matrix products: 217 us -> none  [the longest x52 47 us: product(): return jnp.dot(left, right, preferred_element_type=jnp.float32)]
    unnamed x10 -> x0, blocking collectives: 204 us -> none
    unnamed x1738 -> x37, local copies, waits for them, and re-layouts: 123 us -> 10.3 us
    unnamed x43 -> x0, starting transfers between devices: 101 us -> none
    unnamed x63 -> x0, waiting for transfers between devices: 87.5 us -> none
  transfers between devices with their start and end apart: 60 -> 0, of which waited for: 16 -> 0; matrix products, arithmetic and copies ran while one was open for 19% -> 0% of each run, Pallas kernels for 0% -> 0%
where the time goes in v1:
time: 271 us; the launch traced here: 270 us
  Pallas kernels  223 us (82%)
  local copies, waits for them, and re-layouts  35 us (13%)
  other arithmetic  10.8 us (4%)
    pallas_call x1, Pallas kernels, fast_shards(): pl.pallas_call(layers, out_shape=(jax.ShapeDtypeStruct((BLOCKS, shard, wi...  223 us
    unnamed x37, local copies, waits for them, and re-layouts  10.3 us

profile of v1, /device:TPU:0, one launch (start us, length us, event | category | flops | bytes accessed | tf_op | source)
XLA Modules:
  0.0 270.2 jit_solution(7828392517955388889)
XLA Ops:
  0.7 0.8 constant_dynamic-slice_fusion.2
  1.5 0.1 copy.62
  1.6 0.1 reshape.219
  1.7 0.7 constant_dynamic-slice_fusion
  2.4 0.1 broadcast_in_dim.5
  2.5 0.6 fusion.17
  3.1 2.6 compare_select_fusion.3
  5.7 0.1 stack_reshape.10
  5.8 0.1 stack_reshape.11
  5.9 0.7 constant_dynamic-slice_fusion.1
  6.6 0.7 gt.12
  7.3 0.1 copy.63
  7.4 0.1 copy.82
  7.5 0.1 stack_reshape.9
  7.6 0.6 pad.48.id_col
  8.2 1.3 select_maximum_fusion.bias
  9.6 0.1 copy.83
  9.7 0.6 pad.47.clone.id_row
  10.3 0.9 copy.55
  11.2 0.8 fusion.16
  12.0 0.1 copy.79
  12.1 0.1 copy.78
  12.2 0.8 slice_bitcast_fusion.8
  13.1 0.6 pad_maximum_fusion.2.psh
  13.7 0.9 slice_bitcast_fusion.17
  14.6 0.8 and_convert_fusion.1.tmask
  15.3 0.9 copy.61
  16.3 0.7 pad.40.cot
  17.0 0.2 copy.58
  17.3 0.8 reshape.216.hid0
  18.1 1.6 and_convert_fusion.cmask
  19.7 0.8 fusion
  20.5 0.7 bitcast_dynamic-update-slice_fusion.3
  21.2 0.7 bitcast_dynamic-update-slice_fusion.1
  21.8 0.8 fusion.1
  22.6 0.8 fusion.2
  23.4 0.7 bitcast_dynamic-update-slice_fusion.2
  24.1 0.7 bitcast_dynamic-update-slice_fusion.wsh
  24.7 0.6 constant_dynamic-slice_fusion.3
  25.3 0.1 copy.81
  25.4 1.0 pad.39.clone
  26.5 223.4 %shard_map.314 = (f32[7,96,768]{2,1,0:T(8,128)}, f32[2,40,768]{2,1,0:T(8,128)}, f32[2,40,768]{2,1,0:T(8,128)}, bf16[2,640,192]{2,1,0:T(8,128)(2,1)}, f32[96,512]...) custom-call(bf16[7,96,768]{2,1,0:T(8,128)(2,1)} %bitcast_dynamic-update-slice_fusion.wsh, ...), custom_call_target="tpu_custom_call" | custom-call | tf_op jit(solution)/shard_map/pallas_call | solution.py:1486
  249.9 0.8 slice_reduce_fusion
  250.7 0.1 reshape_squeeze.12
  250.8 0.7 copy.72
  251.4 1.3 slice.123
  252.8 1.3 slice.122
  254.0 1.3 slice.120
  255.4 1.5 slice.121
  256.9 1.0 reshape.223
  257.9 0.9 copy.71
  258.8 1.6 copy.87
  260.4 1.1 slice_bitcast_fusion.5
  261.5 0.8 copy.77
  262.4 0.7 copy.75
  263.1 0.9 copy.73
  264.0 1.1 slice.129
  265.1 1.5 copy_convert_fusion
  266.7 1.0 slice_bitcast_fusion
  267.7 0.1 copy.68
  267.8 0.2 copy.69
  268.1 1.1 copy.76
  269.1 0.1 copy.67
  269.3 0.9 copy.74
  (41 shorter events, 0.5 us)
Async XLA Ops:
  0.7 16.4 %copy-start = (bf16[4,2,40,768]{3,2,1,0:T(8,128)(2,1)S(1)}, bf16[4,2,40,768]{3,2,1,0:T(8,128)(2,1)}, u32[]{:S(2)}) copy-start(bf16[4,2,40,768]{3,2,1,0:T(8,128)(2,1)} %param.19) | copy-start | bytes 1474564
  0.7 13.8 %copy-start.9 = (s32[160]{0:T(256)}, s32[160]{0:T(256)S(1)}, u32[]{:S(2)}) copy-start(s32[160]{0:T(256)S(1)} %and_select_fusion.4) | copy-start | bytes 1924
  12.1 6.0 %copy-start.3 = (bf16[6,96,192]{2,1,0:T(8,128)(2,1)S(1)}, bf16[6,96,192]{2,1,0:T(8,128)(2,1)}, u32[]{:S(2)}) copy-start(bf16[6,96,192]{2,1,0:T(8,128)(2,1)} %param.29) | copy-start | bytes 663556
  16.3 4.2 %copy-start.5 = (bf16[96,768]{1,0:T(8,128)(2,1)S(1)}, bf16[96,768]{1,0:T(8,128)(2,1)}, u32[]{:S(2)}) copy-start(bf16[96,768]{1,0:T(8,128)(2,1)} %param.27) | copy-start | bytes 442372
  16.3 4.8 %copy-start.6 = (bf16[768,96]{0,1:T(8,128)(2,1)S(1)}, bf16[768,96]{0,1:T(8,128)(2,1)}, u32[]{:S(2)}) copy-start(bf16[768,96]{0,1:T(8,128)(2,1)} %param.28) | copy-start | bytes 442372
  17.3 7.4 %copy-start.2 = (bf16[4,2,145,768]{3,1,2,0:T(2,128)(2,1)S(1)}, bf16[4,2,145,768]{3,1,2,0:T(2,128)(2,1)}, u32[]{:S(2)}) copy-start(bf16[4,2,145,768]{3,1,2,0:T(2,128)(2,1)} %param.21) | copy-start | bytes 5345284
  18.1 5.3 %copy-start.7 = (bf16[96,768]{1,0:T(8,128)(2,1)S(1)}, bf16[96,768]{1,0:T(8,128)(2,1)}, u32[]{:S(2)}) copy-start(bf16[96,768]{1,0:T(8,128)(2,1)} %param.31) | copy-start | bytes 442372
  18.1 6.0 %copy-start.8 = (bf16[768,96]{0,1:T(8,128)(2,1)S(1)}, bf16[768,96]{0,1:T(8,128)(2,1)}, u32[]{:S(2)}) copy-start(bf16[768,96]{0,1:T(8,128)(2,1)} %param.32) | copy-start | bytes 442372
  249.8 13.2 %copy-start.4 = (f32[2,40,768]{2,1,0:T(8,128)S(1)}, f32[2,40,768]{2,1,0:T(8,128)}, u32[]{:S(2)}) copy-start(f32[2,40,768]{2,1,0:T(8,128)} %get-tuple-element.26) | copy-start | bytes 737284
  263.1 3.5 %copy-start.1 = (f32[7,96,768]{2,1,0:T(8,128)S(1)}, f32[7,96,768]{2,1,0:T(8,128)}, u32[]{:S(2)}) copy-start(f32[7,96,768]{2,1,0:T(8,128)} %get-tuple-element.28) | copy-start | bytes 6193156

commit v2 on v1

--- a/solution.py
+++ b/solution.py
@@ -611,7 +611,7 @@
 BLOCKS = 7
 BACK_ORDER = (M_DOWN, M_UP, M_CROSS, M_SELF, T_DOWN, T_UP, T_ATT)
 SLOTS = 4
-IMAGE_PAD = 160
+IMAGE_PAD = 16
 NORMS = 5
 
 
@@ -648,16 +648,42 @@
 
 
 def layers(
-    wsh, psh, bias, hid0, img, cot, tmask, cmask, id_row, id_col, gains, offs,
+    lengths, *arrays
+):
+    sources, arrays = arrays[:LOADS], arrays[LOADS:]
+    outputs, arrays = arrays[:7], arrays[7:]
+    targets, rest = arrays[:LOADS], arrays[LOADS:]
+    layers_body(lengths, sources, targets, *targets, *outputs, *rest)
+
+
+LOADS = 18
+
+
+def layers_body(
+    lengths, sources, targets,
+    text_qkv, text_out, text_up, head_bias, up_bias, text_in, text_down, image_mask, image_in,
+    merge_qkv, merge_out, merge_up, merge_down, gains, offs, image_ids, projections, cot,
     wout, mout, tgout, imout, pjout, lossout, vout,
     G, PJ, H, XH, RSD, SQ, SK, SV, CQ, CK, CV, OA, PS, PC, PRE, ACT, XS, XR, ACC, DZ, DPRE, DQKV, DKV,
-    RC, R2, R1, RZ, BG, CT, MS, TG, IMO, IMS, IMR, IML, CG, CLS, DU, DUW, DPJ, PXS, PXR, V, VR, LS,
-    own_s, z_s, z_r, s1_s, s1_r, s2_s, s2_r, sc_s, sc_r,
+    RC, R2, R1, RZ, BG, CT, MS, TG, IMO, IMS, IMR, IML, tmask, cmask, CG, CLS, DU, DUW, DPJ, PXF, PXS, PXR, LSR, MSB, MRX, V, VR, LS,
+    img,
+    load_s,
+    z_s, z_r, s1_s, s1_r, s2_s, s2_r, sc_s, sc_r,
     b2_s, b2_r, b1_s, b1_r, bc_s, bc_r, bz_s, bz_r,
     x_s, x_r, m_s, m_r, cg_s, cg_r, v_s, v_r,
 ):
-    width = hid0.shape[1]
-    rows = hid0.shape[0]
+    loads = [
+        pltpu.make_async_copy(source, target, load_s.at[i])
+        for i, (source, target) in enumerate(zip(sources, targets))
+        if i != 8
+    ]
+    micro, pairs, tokens, width = text_in.shape
+    half_micro = micro // 2
+    count = half_micro * pairs
+    rows = count * tokens
+    share = tokens // 4
+    images = image_mask.shape[2]
+    image_rows = img.shape[0] // half_micro
     local = width // 4
     heads = local // HEAD_DIM
     quarter = rows // 4
@@ -677,74 +703,105 @@
     to_c = (dp + 1 - 2 * c, z)
     to_z1, to_z2, to_z3 = (dp, z1), (dp, z2), (dp, z3)
 
+    mine, theirs = half_micro * group, half_micro * (1 - group)
+    part = sources[8].at[pl.ds(mine, half_micro)]
+    loads.insert(8, pltpu.make_async_copy(part, image_in, load_s.at[8]))
     barrier = pltpu.get_barrier_semaphore()
     others = [(lax.rem(dp + step, 8), z) for step in range(1, 8)]
     for where in others + [to_z1, to_z2, to_z3]:
         pl.semaphore_signal(barrier, inc=1, device_id=where, device_id_type=MESH)
+    for load in loads:
+        load.start()
+    def attention_block(qkv, out, first):
+        turned = turn(out)
+        return jnp.concatenate([qkv[first], qkv[first + 1], qkv[first + 2], turned], 1)
+
+    def turn(matrix):
+        size = matrix.shape[1]
+        unit = jnp.where(
+            lax.broadcasted_iota(jnp.int32, (size, size), 0)
+            == lax.broadcasted_iota(jnp.int32, (size, size), 1),
+            1.0,
+            0.0,
+        ).astype(BF)
+        return mm_nt(unit, matrix).astype(BF)
+
+    def pack(k):
+        if k == T_ATT:
+            block = attention_block(text_qkv, text_out[...], 0)
+        elif k == T_UP:
+            block = text_up[...]
+        elif k == T_DOWN:
+            block = text_down[...]
+        elif k == M_SELF:
+            block = attention_block(merge_qkv, merge_out[0], 0)
+        elif k == M_CROSS:
+            block = attention_block(merge_qkv, merge_out[1], 3)
+        elif k == M_UP:
+            block = merge_up[...]
+        else:
+            block = merge_down[...]
+        G[k, 0, y, x, c] = block
+
+    loads[0].wait()
+    loads[1].wait()
+    pack(T_ATT)
     pl.semaphore_wait(barrier, 10)
 
-    def own(k):
-        return pltpu.make_async_copy(wsh.at[k], G.at[k, 0, y, x, c], own_s.at[k])
+    def x_first(k, q):
+        return (k + q) % 2 == 0
 
     def hop_z(k):
-        return remote(wsh.at[k], G.at[k, 1, y, x, c], z_s.at[k], z_r.at[k], to_z2)
+        return remote(
+            G.at[k, 0, y, x, c], G.at[k, 1, y, x, c], z_s.at[k], z_r.at[k], to_z2
+        )
 
     def hop_1(k, q):
-        if q == 0:
-            return remote(wsh.at[k], G.at[k, 0, y, x, c], s1_s.at[k, 0], s1_r.at[k, 0], to_x)
-        part = G.at[k, 1, y, x, c]
-        return remote(part, part, s1_s.at[k, 1], s1_r.at[k, 1], to_y)
+        part = G.at[k, q, y, x, c]
+        return remote(
+            part, part, s1_s.at[k, q], s1_r.at[k, q], to_x if x_first(k, q) else to_y
+        )
 
     def hop_2(k, q):
-        part = G.at[k, 0, y, :, c] if q == 0 else G.at[k, 1, :, x, c]
-        return remote(part, part, s2_s.at[k, q], s2_r.at[k, q], to_y if q == 0 else to_x)
+        part = G.at[k, q, y, :, c] if x_first(k, q) else G.at[k, q, :, x, c]
+        return remote(
+            part, part, s2_s.at[k, q], s2_r.at[k, q], to_y if x_first(k, q) else to_x
+        )
 
     def hop_c(k, q):
         part = G.at[k, q, :, :, c]
         return remote(part, part, sc_s.at[k, q], sc_r.at[k, q], to_c)
 
-    p_own = pltpu.make_async_copy(psh, PJ.at[y, x, c], own_s.at[BLOCKS])
-    p_1 = remote(psh, PJ.at[y, x, c], s1_s.at[BLOCKS, 0], s1_r.at[BLOCKS, 0], to_x)
+    own_proj = PJ.at[y, x, c]
+    p_1 = remote(own_proj, own_proj, s1_s.at[BLOCKS, 0], s1_r.at[BLOCKS, 0], to_x)
     p_2 = remote(PJ.at[y, :, c], PJ.at[y, :, c], s2_s.at[BLOCKS, 0], s2_r.at[BLOCKS, 0], to_y)
     p_c = remote(PJ.at[:, :, c], PJ.at[:, :, c], sc_s.at[BLOCKS, 0], sc_r.at[BLOCKS, 0], to_c)
 
     def tick(j):
         k = j
         if k < BLOCKS:
-            own(k).start()
+            if k > 0:
+                pack(k)
             hop_z(k).start()
             hop_1(k, 0).start()
-        elif k == BLOCKS:
-            p_own.start()
-            p_1.start()
         k = j - 1
         if 0 <= k < BLOCKS:
             hop_z(k).wait_recv()
             hop_1(k, 1).start()
         k = j - 2
         if 0 <= k < BLOCKS:
-            own(k).wait()
             for q in range(2):
                 hop_1(k, q).wait_recv()
                 hop_2(k, q).start()
-        elif k == BLOCKS:
-            p_own.wait()
-            p_1.wait_recv()
-            p_2.start()
         k = j - 3
         if 0 <= k < BLOCKS:
             for q in range(2):
                 hop_2(k, q).wait_recv()
                 hop_c(k, q).start()
-        elif k == BLOCKS:
-            p_2.wait_recv()
-            p_c.start()
         k = j - 4
         if 0 <= k < BLOCKS:
             for q in range(2):
                 hop_c(k, q).wait_recv()
-        elif k == BLOCKS:
-            p_c.wait_recv()
 
     def sent_all():
         for k in range(BLOCKS):
@@ -753,9 +810,6 @@
                 hop_1(k, q).wait_send()
                 hop_2(k, q).wait_send()
                 hop_c(k, q).wait_send()
-        p_1.wait_send()
-        p_2.wait_send()
-        p_c.wait_send()
 
     def swap(e):
         return remote(XS.at[e % 2], XR.at[e], x_s.at[e % 2], x_r.at[e], to_z1)
@@ -770,21 +824,88 @@
         swap(e).wait_recv()
         return XS[e % 2].astype(F32) + XR[e].astype(F32)
 
-    bias_copy = remote(bias, BG.at[1], m_s.at[0], m_r.at[0], to_z2)
+    for load in loads[2:5]:
+        load.wait()
+    BG[0, 0:6, 0:local] = head_bias[...]
+    BG[0, 6:8, :] = up_bias[...]
+    bias_copy = remote(BG.at[0], BG.at[1], m_s.at[0], m_r.at[0], to_z2)
+    cot_copies = [
+        remote(cot.at[pl.ds(mine, half_micro)], CT.at[z], m_s.at[1], m_r.at[1], to_z1),
+        remote(cot.at[pl.ds(theirs, half_micro)], CT.at[z], m_s.at[2], m_r.at[2], to_z2),
+        remote(cot.at[pl.ds(theirs, half_micro)], CT.at[z], m_s.at[3], m_r.at[3], to_z3),
+    ]
+
+    def pair_of(index):
+        side = lax.rem(lax.div(index, share * pairs), half_micro)
+        return side * pairs + lax.rem(index, pairs)
+
+    def token_of(index):
+        part = lax.div(index, share * count)
+        return part * share + lax.div(lax.rem(index, share * pairs), pairs)
+
+    def iota(shape, axis):
+        return lax.broadcasted_iota(jnp.int32, shape, axis)
+
+    def image_inputs():
+        for n in range(half_micro):
+            start, held = n * image_rows, images * pairs
+            for low in range(0, image_rows, IMAGE_PAD):
+                known = [
+                    image_in[n, t]
+                    for t in range(low // pairs, min((low + IMAGE_PAD) // pairs, images))
+                ]
+                missing = IMAGE_PAD - pairs * len(known)
+                if missing:
+                    known.append(jnp.zeros((missing, width), BF))
+                block = jnp.concatenate([part.astype(F32) for part in known], 0)
+                img[start + low : start + low + IMAGE_PAD, :] = block.astype(BF)
+
+    def inputs():
+        whole = [text_in[mine + n // pairs, n % pairs].astype(F32) for n in range(count)]
+        whole = jnp.concatenate(whole, 0).astype(BF)
+        to, place = iota((rows, rows), 0), iota((rows, rows), 1)
+        order = jnp.where(place == pair_of(to) * tokens + token_of(to), 1.0, 0.0).astype(BF)
+        H[0] = mm(order, whole).astype(BF)
+        index = iota((1, rows), 1)
+        limit = jnp.zeros((1, rows), jnp.int32)
+        for n in range(count):
+            limit = jnp.where(
+                pair_of(index) == n, lengths[n % pairs, mine + n // pairs], limit
+            )
+        live = jnp.where(token_of(index) < limit, 1.0, 0.0)
+        tmask[...] = jnp.where(pair_of(to) == pair_of(place), live, 0.0)
+        live = []
+        for n in range(half_micro):
+            known = jnp.where(image_mask[mine + n] > 0, 1.0, 0.0)
+            row = 0.0
+            for p in range(pairs):
+                size = (images, image_rows)
+                to = iota(size, 1)
+                fits = (lax.div(to, pairs) == iota(size, 0)) & (lax.rem(to, pairs) == p)
+                part = jnp.broadcast_to(known[p : p + 1, :], (8, images)).astype(BF)
+                row += mm(part, jnp.where(fits, 1.0, 0.0).astype(BF))
+            live.append(row[0:1, :])
+        live = jnp.concatenate(live, 1)
+        size = (rows, half_micro * image_rows)
+        to = iota(size, 1)
+        of = lax.div(to, image_rows) * pairs + lax.rem(to, pairs)
+        cmask[...] = jnp.where(pair_of(iota(size, 0)) == of, live, 0.0)
+
+    tick(0)
     bias_copy.start()
-    BG[0] = bias[...]
-    cot_copies = [
-        remote(cot.at[group], CT.at[z], m_s.at[1], m_r.at[1], to_z1),
-        remote(cot.at[1 - group], CT.at[z], m_s.at[2], m_r.at[2], to_z2),
-        remote(cot.at[1 - group], CT.at[z], m_s.at[3], m_r.at[3], to_z3),
-    ]
-
-    for j in range(4):
-        tick(j)
+    tick(1)
+    for load in loads[5:]:
+        load.wait()
+    inputs()
+    tick(2)
+    image_inputs()
+    PJ[y, x, c, :, 0 : PJ.shape[-1] // 2] = projections[0]
+    PJ[y, x, c, :, PJ.shape[-1] // 2 :] = projections[1]
+    tick(3)
     bias_copy.wait()
     for copy in cot_copies:
         copy.start()
-    CT[z] = cot[group]
+    CT[z] = cot[pl.ds(mine, half_micro)]
 
     def weight(k, q, lo, hi):
         return G[k, q, :, :, :, :, lo:hi].reshape(width, hi - lo)
@@ -879,7 +1000,6 @@
 
         lax.fori_loop(0, 2, part, 0)
 
-    H[0] = hid0[...]
     tick(4)
     self_attention(T_ATT, 0, 0)
     swap_start(0)
@@ -893,15 +1013,14 @@
     settle_forward(1)
 
     def summary_rows():
-        spot = lax.broadcasted_iota(jnp.int32, (8, rows), 0)
-        place = lax.broadcasted_iota(jnp.int32, (8, rows), 1)
-        pick = jnp.where((place == spot * (quarter // 4)) & (spot < 4), 1.0, 0.0).astype(BF)
-        text_rows = mm(pick, H[2])
-        spot = lax.broadcasted_iota(jnp.int32, (8, img.shape[0]), 0)
-        place = lax.broadcasted_iota(jnp.int32, (8, img.shape[0]), 1)
-        pick = jnp.where((place == spot * IMAGE_PAD) & (spot < 4), 1.0, 0.0).astype(BF)
-        image_rows = mm(pick, img[...])
-        CLS[...] = jnp.concatenate([text_rows, image_rows], 0).astype(BF)
+        def pick(size, step):
+            spot, place = iota((8, size), 0), iota((8, size), 1)
+            fits = place == lax.div(spot, pairs) * step + lax.rem(spot, pairs)
+            return jnp.where(fits & (spot < count), 1.0, 0.0).astype(BF)
+
+        text_rows = mm(pick(rows, share * pairs), H[2])
+        image_cls = mm(pick(img.shape[0], image_rows), img[...])
+        CLS[...] = jnp.concatenate([text_rows, image_cls], 0).astype(BF)
         CG[dp] = CLS[...]
 
     summary_rows()
@@ -919,17 +1038,15 @@
     swap_start(3)
     tick(9)
     settle_forward(3)
+    p_1.start()
     feed_up(M_UP, 4, 1)
     tick(10)
     feed_down(M_DOWN, 1)
     swap_start(4)
-    tick(11)
-    merged = settle_forward(4)
-    MS[...] = merged.reshape(4, quarter, width)
-    mout[group] = MS[z]
-    merged_copy = remote(MS.at[z2], mout.at[group], m_s.at[4], m_r.at[4], to_z2)
-    merged_copy.start()
+    p_1.wait()
+    p_2.start()
     sent_all()
+    V[...] = jnp.zeros_like(V)
 
     def back_c(k, q):
         slot = BACK_ORDER.index(k) % SLOTS
@@ -938,12 +1055,16 @@
         )
 
     def back_2(k, q):
-        part = G.at[k, 0, 1 - y, :, c] if q == 0 else G.at[k, 1, :, 1 - x, c]
-        return remote(part, R2.at[k, q], b2_s.at[k, q], b2_r.at[k, q], to_y if q == 0 else to_x)
+        part = G.at[k, q, 1 - y, :, c] if x_first(k, q) else G.at[k, q, :, 1 - x, c]
+        return remote(
+            part, R2.at[k, q], b2_s.at[k, q], b2_r.at[k, q], to_y if x_first(k, q) else to_x
+        )
 
     def back_1(k, q):
-        part = G.at[k, 0, y, 1 - x, c] if q == 0 else G.at[k, 1, 1 - y, x, c]
-        return remote(part, R1.at[k, q], b1_s.at[k, q], b1_r.at[k, q], to_x if q == 0 else to_y)
+        part = G.at[k, q, y, 1 - x, c] if x_first(k, q) else G.at[k, q, 1 - y, x, c]
+        return remote(
+            part, R1.at[k, q], b1_s.at[k, q], b1_r.at[k, q], to_x if x_first(k, q) else to_y
+        )
 
     def back_z(k):
         return remote(G.at[k, 1, y, x, c], RZ.at[k], bz_s.at[k], bz_r.at[k], to_z2)
@@ -951,46 +1072,42 @@
     def both(a, b):
         return (a.astype(F32) + b.astype(F32)).astype(BF)
 
-    def back_tick(j):
-        n = j
-        if n < BLOCKS:
-            for q in range(2):
-                back_c(BACK_ORDER[n], q).start()
-        n = j - 1
-        if 0 <= n < BLOCKS:
-            k = BACK_ORDER[n]
-            for q in range(2):
-                back_c(k, q).wait()
-                for a in range(2):
-                    for b in range(2):
-                        G[k, q, a, b, c] = both(G[k, q, a, b, c], RC[n % SLOTS, q, a, b])
-                back_2(k, q).start()
-        n = j - 2
-        if 0 <= n < BLOCKS:
-            k = BACK_ORDER[n]
-            for q in range(2):
-                back_2(k, q).wait()
-                for a in range(2):
-                    if q == 0:
-                        G[k, 0, y, a, c] = both(G[k, 0, y, a, c], R2[k, 0, a])
-                    else:
-                        G[k, 1, a, x, c] = both(G[k, 1, a, x, c], R2[k, 1, a])
-                back_1(k, q).start()
-        n = j - 3
-        if 0 <= n < BLOCKS:
-            k = BACK_ORDER[n]
-            back_1(k, 1).wait()
-            G[k, 1, y, x, c] = both(G[k, 1, y, x, c], R1[k, 1])
-            back_z(k).start()
-            back_1(k, 0).wait()
-            wout[k] = G[k, 0, y, x, c].astype(F32) + R1[k, 0].astype(F32)
-        n = j - 4
-        if 0 <= n < BLOCKS:
-            k = BACK_ORDER[n]
-            back_z(k).wait()
-            wout[k] = wout[k] + RZ[k].astype(F32)
-
-    V[...] = jnp.zeros_like(V)
+    def c_start(n):
+        for q in range(2):
+            back_c(BACK_ORDER[n], q).start()
+
+    def a_step(n):
+        k = BACK_ORDER[n]
+        for q in range(2):
+            back_c(k, q).wait()
+            for a in range(2):
+                for b in range(2):
+                    G[k, q, a, b, c] = both(G[k, q, a, b, c], RC[n % SLOTS, q, a, b])
+            back_2(k, q).start()
+
+    def b_step(n):
+        k = BACK_ORDER[n]
+        for q in range(2):
+            back_2(k, q).wait()
+            for a in range(2):
+                if x_first(k, q):
+                    G[k, q, y, a, c] = both(G[k, q, y, a, c], R2[k, q, a])
+                else:
+                    G[k, q, a, x, c] = both(G[k, q, a, x, c], R2[k, q, a])
+            back_1(k, q).start()
+
+    def d_step(n):
+        k = BACK_ORDER[n]
+        back_1(k, 1).wait()
+        G[k, 1, y, x, c] = both(G[k, 1, y, x, c], R1[k, 1])
+        back_z(k).start()
+        back_1(k, 0).wait()
+        wout[k] = G[k, 0, y, x, c].astype(F32) + R1[k, 0].astype(F32)
+
+    def e_step(n):
+        k = BACK_ORDER[n]
+        back_z(k).wait()
+        wout[k] = wout[k] + RZ[k].astype(F32)
 
     def norm_backward(e, grad):
         xhat = XH[e]
@@ -1013,9 +1130,12 @@
 
     def feed_backward(up, down, e, layer, rounded):
         ACC[...] = jnp.zeros_like(ACC)
+        turned = rounded.T
 
         def part(q, carry):
             grad = mm(rounded, weight(down, q, 0, width))
+            keep_grad(down, q, 0, mm(turned, ACT[layer, q]))
+            back_c(down, q).start()
             pre = PRE[layer, q]
             slope = gelu_parts(pre) + pre * (
                 jnp.exp(-0.5 * pre * pre) * (1.0 / math.sqrt(2.0 * math.pi))
@@ -1024,15 +1144,6 @@
             DPRE[q] = grad
             V[pl.ds(15 + 2 * q + layer, 1), :] = jnp.sum(grad.astype(F32), 0, keepdims=True)
             ACC[...] += mm_nt(grad, weight(up, q, 0, width))
-            return carry
-
-        lax.fori_loop(0, 2, part, 0)
-
-    def feed_down_grad(down, layer, rounded):
-        turned = rounded.T
-
-        def part(q, carry):
-            keep_grad(down, q, 0, mm(turned, ACT[layer, q]))
             return carry
 
         lax.fori_loop(0, 2, part, 0)
@@ -1173,14 +1284,35 @@
         proj = PJ[...].reshape(width, PJ.shape[-1])
         half = proj.shape[1] // 2
         text_rows = CG[:, 0:8, :].reshape(spots, width)
-        image_rows = CG[:, 8:16, :].reshape(spots, width)
+        image_cls = CG[:, 8:16, :].reshape(spots, width)
         raw_t = mm(text_rows, proj[:, :half])
-        raw_w = mm(image_rows, proj[:, half:])
+        raw_w = mm(image_cls, proj[:, half:])
         inv_t = lax.rsqrt(jnp.sum(raw_t * raw_t, -1, keepdims=True) + EPS)
         inv_w = lax.rsqrt(jnp.sum(raw_w * raw_w, -1, keepdims=True) + EPS)
         t, w = raw_t * inv_t, raw_w * inv_w
-        row_key, col_key = id_row[:, 0:1], id_col[0:1, 0:spots]
-        row_batch, col_batch = id_row[:, 1:2], id_col[1:2, 0:spots]
+        known = image_ids.shape[1]
+
+        def spread_of(shape, spot_axis, batch):
+            spot = lax.broadcasted_iota(jnp.int32, shape, spot_axis)
+            pair = lax.broadcasted_iota(jnp.int32, shape, 1 - spot_axis)
+            fits = (lax.div(spot, 8) == lax.div(pair, pairs)) & (
+                lax.rem(spot, 8) == batch * pairs + lax.rem(pair, pairs)
+            )
+            return jnp.where(fits, 1.0, 0.0)
+
+        row_key, col_key = 0.0, 0.0
+        for n in range(half_micro):
+            drawn = image_ids[pl.ds(mine + n, 1), :].astype(F32)
+            drawn = jnp.broadcast_to(drawn, (8, known))
+            row_key += mm_exact(spread_of((spots, known), 0, n), drawn, NT)[:, 0:1]
+            col_key += mm_exact(drawn, spread_of((known, spots), 1, n), NN)[0:1, :]
+
+        def batch_of(axis):
+            shape = (spots, 1) if axis == 0 else (1, spots)
+            place = lax.rem(lax.broadcasted_iota(jnp.int32, shape, axis), 8)
+            return jnp.where(place < count, lax.div(place, pairs), -1)
+
+        row_batch, col_batch = batch_of(0), batch_of(1)
         live = row_batch == col_batch
         same = jnp.where(live & (row_key == col_key), 1.0, 0.0)
         target = same / jnp.sum(same, 1, keepdims=True)
@@ -1202,69 +1334,128 @@
         grad_w = mm_exact(over_t, t, TN) + mm_exact(over_w, t, NN)
         grad_t = (grad_t - t * jnp.sum(t * grad_t, -1, keepdims=True)) * inv_t
         grad_w = (grad_w - w * jnp.sum(w * grad_w, -1, keepdims=True)) * inv_w
-        valid = id_row[:, 2:3]
+        valid = jnp.where(row_batch >= 0, 1.0, 0.0)
         grad_t, grad_w = grad_t * valid, grad_w * valid
         DU[...] = grad_t.reshape(8, 8, half)
         DUW[...] = grad_w.reshape(8, 8, half)
         LS[...] = jnp.broadcast_to(loss, (spots, 128)).reshape(8, 8, 128)
-        DPJ[:, :, 0:half] = mm_exact(text_rows.astype(F32), grad_t, TN).reshape(
-            8, width // 8, half
-        )
-        DPJ[:, :, half:] = mm_exact(image_rows.astype(F32), grad_w, TN).reshape(
-            8, width // 8, half
-        )
-        PXS[0 : width // 8, :] = DPJ[dp]
-        PXS[width // 8 :, :] = jnp.concatenate([LS[dp]] * (PXS.shape[1] // 128), 1)
+        size = (8, width // 8, half)
+        DPJ[...] = mm_exact(text_rows.astype(F32), grad_t, TN).reshape(size)
+        PXF[:, 0:half] = DPJ[dp]
+        DPJ[...] = mm_exact(image_cls.astype(F32), grad_w, TN).reshape(size)
+        PXF[:, half:] = DPJ[dp]
+        PXS[...] = PXF[...].astype(BF)
 
     pair_copy = remote(PXS, PXR, m_s.at[5], m_r.at[5], to_z2)
+    loss_copy = remote(LS.at[dp], LSR, m_s.at[9], m_r.at[9], to_z2)
+
+    def image_extra(place):
+        part = PJ[lax.div(place, 2), lax.rem(place, 2), :, :, PJ.shape[-1] // 2 :]
+        return mm_exact(DUW[dp], part.reshape(local, PJ.shape[-1] // 2).astype(F32), NT)
+
+    image_copy = remote(IMS, IMR, m_s.at[6], m_r.at[6], to_z1)
+    image_last = remote(IML, imout.at[group], m_s.at[7], m_r.at[7], to_z2)
+
+    def image_finish():
+        extra = jnp.concatenate([image_extra(z), image_extra(z2)], 1)
+        spot = iota((8, 2 * local), 0)
+        image_copy.wait()
+        IMO[...] += IMR[...].astype(F32)
+        for n in range(count):
+            start = n // pairs * image_rows
+            span = slice(start, start + 8)
+            IMO[span, :] = IMO[span, :] + jnp.where(
+                spot == n % pairs, extra[n : n + 1, :], 0.0
+            )
+
+        def side_by_side(low):
+            parts = [
+                IMO[n * image_rows : (n + 1) * image_rows, low : low + local]
+                for n in range(half_micro)
+            ]
+            return jnp.concatenate(parts, 1).astype(BF)
+
+        IML[...] = side_by_side(local)
+        image_last.start()
+        imout[group] = side_by_side(0)
 
     for copy in cot_copies:
         copy.wait()
-    grad = jnp.concatenate([CT[i].astype(F32)[:quarter] for i in range(4)], 0)
-    rounded = norm_backward(4, grad)
+    DZ[...] = jnp.concatenate(
+        [
+            CT[i, n, t].astype(F32)
+            for i in range(4)
+            for n in range(half_micro)
+            for t in range(share)
+        ],
+        0,
+    )
+    merged = settle_forward(4)
+    rounded = norm_backward(4, DZ[...])
     feed_backward(M_UP, M_DOWN, 4, 1, rounded)
+    MS[...] = merged.reshape(4, quarter, width)
     swap_start(5)
-    feed_down_grad(M_DOWN, 1, rounded)
-    back_tick(0)
     feed_up_grad(M_UP, 4)
-    back_tick(1)
+    c_start(1)
+    a_step(0)
+    mout[group] = MS[z]
+    MSB[0] = MS[z2].astype(BF)
+    merged_copy = remote(MSB.at[0], MRX.at[0], m_s.at[4], m_r.at[4], to_z2)
+    text_copy = remote(MSB.at[1], MRX.at[1], m_s.at[8], m_r.at[8], to_z2)
+    merged_copy.start()
+    p_2.wait()
+    p_c.start()
     rounded = norm_backward(3, DZ[...] + swap_sum(5))
+    a_step(1)
     cross_backward(rounded)
     swap_start(6)
+    b_step(0)
     IMS[...] = image_columns(z1, z3).astype(BF)
-    image_copy = remote(IMS, IMR, m_s.at[6], m_r.at[6], to_z1)
-    image_copy.start()
     IMO[...] = image_columns(z, z2)
     cross_grad(rounded)
-    back_tick(2)
+    c_start(2)
+    b_step(1)
     rounded = norm_backward(2, DZ[...] + swap_sum(6))
+    a_step(2)
+    image_copy.start()
+    d_step(0)
     self_backward(M_SELF, 1, rounded)
     swap_start(7)
     self_grad(M_SELF, 2, 1, rounded)
-    back_tick(3)
+    c_start(3)
+    d_step(1)
+    b_step(2)
+    a_step(3)
+    p_c.wait()
     for copy in summary:
         copy.wait()
     contrast()
     pair_copy.start()
+    loss_copy.start()
 
     proj_text = PJ[:, :, :, :, 0 : PJ.shape[-1] // 2].reshape(width, PJ.shape[-1] // 2)
     extra = mm_exact(DU[dp], proj_text.astype(F32), NT)
     place = lax.broadcasted_iota(jnp.int32, (rows, width), 0)
     grad = DZ[...] + swap_sum(7)
-    for n in range(4):
-        grad = grad + jnp.where(place == n * (quarter // 4), extra[n : n + 1, :], 0.0)
+    for n in range(count):
+        grad = grad + jnp.where(
+            place == n // pairs * share * pairs + n % pairs, extra[n : n + 1, :], 0.0
+        )
     rounded = norm_backward(1, grad)
     feed_backward(T_UP, T_DOWN, 1, 0, rounded)
     swap_start(8)
-    feed_down_grad(T_DOWN, 0, rounded)
-    back_tick(4)
+    d_step(2)
     feed_up_grad(T_UP, 1)
-    back_tick(5)
+    c_start(5)
+    b_step(3)
+    a_step(4)
+    image_finish()
     rounded = norm_backward(0, DZ[...] + swap_sum(8))
+    a_step(5)
+    e_step(0)
+    e_step(1)
     self_backward(T_ATT, 0, rounded)
     swap_start(9)
-    self_grad(T_ATT, 0, 0, rounded)
-    back_tick(6)
 
     stat_to = (to_c, to_x, to_y, to_z2)
 
@@ -1272,46 +1463,109 @@
         return remote(V, VR.at[i], v_s.at[i], v_r.at[i], stat_to[i])
 
     stat_copy(0).start()
-
-    def image_extra(place):
-        part = PJ[lax.div(place, 2), lax.rem(place, 2), :, :, PJ.shape[-1] // 2 :]
-        return mm_exact(DUW[dp], part.reshape(local, PJ.shape[-1] // 2).astype(F32), NT)
-
-    image_copy.wait()
-    IMO[...] += IMR[...].astype(F32)
-    extra = jnp.concatenate([image_extra(z), image_extra(z2)], 1)
-    first_row = lax.broadcasted_iota(jnp.int32, (8, 2 * local), 0) == 0
-    for n in range(4):
-        span = slice(n * IMAGE_PAD, n * IMAGE_PAD + 8)
-        IMO[span, :] = IMO[span, :] + jnp.where(first_row, extra[n : n + 1, :], 0.0)
-    imout[group] = IMO[:, :local].astype(BF)
-    IML[...] = IMO[:, local:].astype(BF)
-    image_last = remote(IML, imout.at[group], m_s.at[7], m_r.at[7], to_z2)
-    image_last.start()
+    d_step(3)
+    b_step(4)
+    self_grad(T_ATT, 0, 0, rounded)
+    c_start(6)
+    b_step(5)
+    a_step(6)
+    d_step(4)
 
     grad = DZ[...] + swap_sum(9)
     TG[...] = grad.reshape(4, quarter, width)
+    MSB[1] = TG[z2].astype(BF)
+    text_copy.start()
     tgout[group] = TG[z]
-    text_copy = remote(TG.at[z2], tgout.at[group], m_s.at[8], m_r.at[8], to_z2)
-    text_copy.start()
-    for i in range(4):
-        back_tick(7 + i)
+    def stat_step(i):
         stat_copy(i).wait()
         if i < 3:
             V[...] = V[...] + VR[i]
             stat_copy(i + 1).start()
+
+    stat_step(0)
+    d_step(5)
+    stat_step(1)
+    b_step(6)
+    e_step(2)
+    stat_step(2)
+    e_step(3)
+    e_step(4)
+    d_step(6)
+    stat_step(3)
     vout[0:15, :] = V[0:15, :] + VR[3, 0:15, :]
     vout[16:18, :] = V[15:17, :] + VR[3, 17:19, :]
     vout[24:30, :] = V[19:25, :] + VR[3, 25:31, :]
+    e_step(5)
     pair_copy.wait()
-    pjout[...] = PXS[0 : width // 8, :] + PXR[0 : width // 8, :]
-    lossout[group] = PXS[width // 8 :, 0:128]
-    lossout[1 - group] = PXR[width // 8 :, 0:128]
+    loss_copy.wait()
+    pjout[...] = PXF[...] + PXR[...].astype(F32)
+    lossout[group] = LS[dp]
+    lossout[1 - group] = LSR[...]
     image_last.wait()
     text_copy.wait()
+    tgout[1 - group] = MRX[1].astype(F32)
     merged_copy.wait()
+    mout[1 - group] = MRX[0].astype(F32)
     swap(8).wait_send()
     swap(9).wait_send()
+    e_step(6)
+
+
+def unpack(
+    wout, mout, tgout, imout, pjout, lossout, vout,
+    merged, loss, text_grad, image_grad, text_qkv, text_out, text_up, text_down, merge_qkv,
+    merge_out, merge_up, merge_down, projections, gains, offs, head_bias, up_bias,
+):
+    micro, share, pairs, width = merged.shape
+    images = image_grad.shape[1]
+    local = width // 4
+    half_micro = micro // 2
+    image_rows = imout.shape[1]
+
+    for m in range(micro):
+        side, start = m // half_micro, m % half_micro * share * pairs
+        for t in range(share):
+            span = slice(start + t * pairs, start + (t + 1) * pairs)
+            merged[m, t] = mout[side, span, :]
+            text_grad[m, t] = tgout[side, span, :]
+        start = m % half_micro * local
+        for low in range(0, images * pairs, IMAGE_PAD):
+            block = imout[side, low : low + IMAGE_PAD, start : start + local].astype(F32)
+            for t in range(low // pairs, min((low + IMAGE_PAD) // pairs, images)):
+                image_grad[m, t] = block[t * pairs - low : (t + 1) * pairs - low]
+
+    row = lax.broadcasted_iota(jnp.int32, (pairs, micro), 0)
+    column = lax.broadcasted_iota(jnp.int32, (pairs, micro), 1)
+    known = jnp.zeros((pairs, micro), F32)
+    for m in range(micro):
+        for p in range(pairs):
+            n = m % half_micro * pairs + p
+            known = jnp.where(
+                (column == m) & (row == p), lossout[m // half_micro, n : n + 1, 0:1], known
+            )
+    loss[...] = known
+
+    def block(k, place, out):
+        out[...] = wout[k, :, place * local : (place + 1) * local]
+
+    for i in range(3):
+        block(T_ATT, i, text_qkv.at[i])
+        block(M_SELF, i, merge_qkv.at[i])
+        block(M_CROSS, i, merge_qkv.at[3 + i])
+    text_out[...] = wout[T_ATT, :, 3 * local :].T
+    merge_out[0] = wout[M_SELF, :, 3 * local :].T
+    merge_out[1] = wout[M_CROSS, :, 3 * local :].T
+    text_up[...] = wout[T_UP]
+    merge_up[...] = wout[M_UP]
+    text_down[...] = wout[T_DOWN]
+    merge_down[...] = wout[M_DOWN]
+    half = pjout.shape[1] // 2
+    projections[0] = pjout[:, :half]
+    projections[1] = pjout[:, half:]
+    gains[...] = vout[0:5, :]
+    offs[...] = vout[5:15, :]
+    up_bias[...] = vout[16:18, :]
+    head_bias[...] = vout[24:30, 0:local]
 
 
 def fast_shards(
@@ -1339,8 +1593,6 @@
     images = image_embeds.shape[2]
     data_parts = lax.axis_size("dp")
     model_parts = lax.axis_size("mp")
-    z = lax.axis_index("mp")
-    group = z // 2
     local = width // model_parts
     shard = width // data_parts
     half_micro = micro // 2
@@ -1349,67 +1601,8 @@
     share = tokens // model_parts
     rows = count * tokens
     quarter = rows // model_parts
-
-    def mine(array):
-        return lax.dynamic_slice_in_dim(array, group * half_micro, half_micro, 0)
-
-    def attention_block(qkv, out):
-        return jnp.concatenate([qkv[0], qkv[1], qkv[2], out.T], 1)
-
-    wsh = jnp.stack(
-        [
-            attention_block(text_qkv, text_out),
-            text_up,
-            text_down.T,
-            attention_block(merge_qkv[:3], merge_out[0]),
-            attention_block(merge_qkv[3:], merge_out[1]),
-            merge_up,
-            merge_down.T,
-        ]
-    )
-    psh = jnp.concatenate([projections[0], projections[1]], 1)
-    bias = jnp.concatenate(
-        [jnp.pad(head_biases, ((0, 0), (0, width - local))), up_biases], 0
-    )
-    hid0 = (
-        mine(text_embeds)
-        .reshape(half_micro, pairs, model_parts, share, width)
-        .transpose(2, 0, 1, 3, 4)
-        .reshape(rows, width)
-    )
-    img = jnp.pad(
-        mine(image_embeds), ((0, 0), (0, 0), (0, IMAGE_PAD - images), (0, 0))
-    ).reshape(count * IMAGE_PAD, width)
-    cot = jnp.pad(
-        out_cot.reshape(groups, quarter, width), ((0, 0), (0, 48 - quarter), (0, 0))
-    )
-    lengths = mine(text_lengths).reshape(count)
-    place = jnp.arange(rows)
-    pair_of = (place // share) % count
-    token_of = (place // quarter) * share + place % share
-    text_live = token_of < lengths[pair_of]
-    tmask = ((pair_of[:, None] == pair_of[None, :]) & text_live[None, :]).astype(jnp.float32)
-    image_live = jnp.pad(
-        mine(image_mask), ((0, 0), (0, 0), (0, IMAGE_PAD - images))
-    ).reshape(count * IMAGE_PAD)
-    image_of = jnp.arange(count * IMAGE_PAD) // IMAGE_PAD
-    cmask = ((pair_of[:, None] == image_of[None, :]) & (image_live > 0)[None, :]).astype(
-        jnp.float32
-    )
-    ids = mine(image_ids).reshape(half_micro, data_parts, pairs).transpose(1, 0, 2)
-    batch = jnp.broadcast_to(jnp.arange(half_micro)[None, :, None], ids.shape)
-    live = jnp.ones_like(ids)
-
-    def spots(array, fill):
-        array = array.reshape(data_parts, count)
-        return jnp.pad(
-            array, ((0, 0), (0, 8 - count)), constant_values=fill
-        ).reshape(data_parts * 8)
-
-    table = jnp.stack([spots(ids, 0), spots(batch, -1), spots(live, 0)]).astype(jnp.float32)
-    id_row = jnp.pad(table.T, ((0, 0), (0, 125)))
-    id_col = jnp.pad(table, ((0, 5), (0, 128 - data_parts * 8)))
-
+    proj_width = 2 * projections.shape[2]
+    image_rows = -(-images * pairs // IMAGE_PAD) * IMAGE_PAD
     vmem = pl.BlockSpec(memory_space=pltpu.VMEM)
 
     def sem(*shape):
@@ -1419,9 +1612,17 @@
         return pltpu.VMEM(shape, dtype)
 
     grid = (2, 2, 2, shard)
+    inputs = (
+        text_qkv, text_out, text_up, head_biases, up_biases, text_embeds, text_down.T, image_mask,
+        image_embeds.transpose(0, 2, 1, 3), merge_qkv, merge_out, merge_up, merge_down.T,
+        norm_gains, offsets, image_ids, projections, out_cot.transpose(0, 2, 1, 3),
+    )
+    held = [pltpu.VMEM(array.shape, array.dtype) for array in inputs]
+    held[8] = pltpu.VMEM((half_micro, images, pairs, width), BF)
     scratch = [
+        *held,
         buf(BLOCKS, 2, *grid, width),
-        buf(*grid, psh.shape[1]),
+        buf(*grid, proj_width),
         buf(NORMS, rows, width),
         buf(NORMS, rows, width, dtype=F32),
         buf(NORMS, rows, 1, dtype=F32),
@@ -1429,11 +1630,11 @@
         buf(2, 2, rows, local),
         buf(2, 2, rows, local),
         buf(2, rows, local),
-        buf(2, count * IMAGE_PAD, local),
-        buf(2, count * IMAGE_PAD, local),
+        buf(2, half_micro * image_rows, local),
+        buf(2, half_micro * image_rows, local),
         buf(3, 2, rows, local),
         buf(2, 2, local // HEAD_DIM, rows, rows),
-        buf(2, local // HEAD_DIM, rows, count * IMAGE_PAD),
+        buf(2, local // HEAD_DIM, rows, half_micro * image_rows),
         buf(2, 2, rows, width, dtype=F32),
         buf(2, 2, rows, width),
         buf(2, rows, width),
@@ -1442,30 +1643,37 @@
         buf(rows, width, dtype=F32),
         buf(2, rows, width),
         buf(2, rows, 3 * local),
-        buf(2, count * IMAGE_PAD, 2 * local),
+        buf(2, half_micro * image_rows, 2 * local),
         buf(SLOTS, 2, 2, 2, shard, width),
         buf(BLOCKS, 2, 2, shard, width),
         buf(BLOCKS, 2, shard, width),
         buf(BLOCKS, shard, width),
         buf(2, 8, width, dtype=F32),
-        buf(model_parts, 48, width),
+        buf(model_parts, half_micro, share, pairs, width),
         buf(model_parts, quarter, width, dtype=F32),
         buf(model_parts, quarter, width, dtype=F32),
-        buf(count * IMAGE_PAD, 2 * local, dtype=F32),
-        buf(count * IMAGE_PAD, 2 * local),
-        buf(count * IMAGE_PAD, 2 * local),
-        buf(count * IMAGE_PAD, local),
+        buf(half_micro * image_rows, 2 * local, dtype=F32),
+        buf(half_micro * image_rows, 2 * local),
+        buf(half_micro * image_rows, 2 * local),
+        buf(image_rows, half_micro * local),
+        buf(rows, rows, dtype=F32),
+        buf(rows, half_micro * image_rows, dtype=F32),
         buf(data_parts, 16, width),
         buf(16, width),
-        buf(data_parts, 8, psh.shape[1] // 2, dtype=F32),
-        buf(data_parts, 8, psh.shape[1] // 2, dtype=F32),
-        buf(data_parts, shard, psh.shape[1], dtype=F32),
-        buf(shard + 8, psh.shape[1], dtype=F32),
-        buf(shard + 8, psh.shape[1], dtype=F32),
+        buf(data_parts, 8, proj_width // 2, dtype=F32),
+        buf(data_parts, 8, proj_width // 2, dtype=F32),
+        buf(data_parts, shard, proj_width // 2, dtype=F32),
+        buf(shard, proj_width, dtype=F32),
+        buf(shard, proj_width),
+        buf(shard, proj_width),
+        buf(8, 128, dtype=F32),
+        buf(2, quarter, width),
+        buf(2, quarter, width),
         buf(32, width, dtype=F32),
         buf(4, 32, width, dtype=F32),
         buf(data_parts, 8, 128, dtype=F32),
-        sem(BLOCKS + 1),
+        buf(half_micro * image_rows, width),
+        sem(LOADS),
         sem(BLOCKS),
         sem(BLOCKS),
         *[sem(BLOCKS + 1, 2) for _ in range(6)],
@@ -1473,67 +1681,60 @@
         *[sem(BLOCKS) for _ in range(2)],
         sem(2),
         sem(2 * NORMS),
-        sem(9),
-        sem(9),
+        sem(10),
+        sem(10),
         sem(data_parts - 1),
         sem(data_parts - 1),
         sem(4),
         sem(4),
     ]
-    inputs = (
-        wsh, psh, bias, hid0, img, cot, tmask, cmask, id_row, id_col, norm_gains, offsets,
-    )
-    wout, mout, tgout, imout, pjout, lossout, vout = pl.pallas_call(
+    packed = pl.pallas_call(
         layers,
         out_shape=(
             jax.ShapeDtypeStruct((BLOCKS, shard, width), F32),
             jax.ShapeDtypeStruct((groups, quarter, width), F32),
             jax.ShapeDtypeStruct((groups, quarter, width), F32),
-            jax.ShapeDtypeStruct((groups, count * IMAGE_PAD, local), BF),
-            jax.ShapeDtypeStruct((shard, psh.shape[1]), F32),
+            jax.ShapeDtypeStruct((groups, image_rows, half_micro * local), BF),
+            jax.ShapeDtypeStruct((shard, proj_width), F32),
             jax.ShapeDtypeStruct((groups, 8, 128), F32),
             jax.ShapeDtypeStruct((32, width), F32),
         ),
-        in_specs=[vmem] * len(inputs),
+        in_specs=[pl.BlockSpec(memory_space=pltpu.SMEM)] + [pl.BlockSpec(memory_space=pl.ANY)] * LOADS,
         out_specs=(vmem,) * 7,
         scratch_shapes=scratch,
         compiler_params=pltpu.CompilerParams(
             collective_id=0, has_side_effects=True, vmem_limit_bytes=63 * 2**20
         ),
-    )(*inputs)
-
-    def parts(block, number):
-        return block.reshape(shard, number, local).transpose(1, 0, 2)
-
-    def text_shape(array):
-        return array.reshape(micro, pairs, share, width)
-
-    split = 3 * local
-    image_grad = (
-        imout.reshape(micro, pairs, IMAGE_PAD, local)[:, :, :images].astype(F32)
-    )
-    loss = lossout[:, :count, 0].reshape(micro, pairs)
-    return (
-        text_shape(mout),
-        loss,
-        text_shape(tgout),
-        image_grad,
-        parts(wout[T_ATT, :, :split], 3),
-        wout[T_ATT, :, split:].T,
-        wout[T_UP],
-        wout[T_DOWN].T,
-        jnp.concatenate(
-            [parts(wout[M_SELF, :, :split], 3), parts(wout[M_CROSS, :, :split], 3)], 0
+    )(text_lengths.T, *inputs)
+
+    def out(*shape):
+        return jax.ShapeDtypeStruct(shape, F32)
+
+    done = pl.pallas_call(
+        unpack,
+        out_shape=(
+            out(micro, share, pairs, width),
+            out(pairs, micro),
+            out(micro, share, pairs, width),
+            out(micro, images, pairs, local),
+            *[
+                out(*array.shape)
+                for array in (
+                    text_qkv, text_out, text_up, text_down.T, merge_qkv, merge_out, merge_up,
+                    merge_down.T, projections, norm_gains, offsets, head_biases, up_biases,
+                )
+            ],
         ),
-        jnp.stack([wout[M_SELF, :, split:].T, wout[M_CROSS, :, split:].T]),
-        wout[M_UP],
-        wout[M_DOWN].T,
-        pjout.reshape(shard, 2, -1).transpose(1, 0, 2),
-        vout[0:5],
-        vout[5:15],
-        vout[24:30, :local],
-        vout[16:18],
-    )
+        in_specs=[vmem] * 7,
+        out_specs=(vmem,) * 17,
+        compiler_params=pltpu.CompilerParams(vmem_limit_bytes=63 * 2**20),
+    )(*packed)
+    done = list(done)
+    for i in (0, 2, 3):
+        done[i] = done[i].transpose(0, 2, 1, 3)
+    for i in (1, 7, 11):
+        done[i] = done[i].T
+    return tuple(done)
 
 
 def solution(mesh):

time: 271 us -> 211 us (0.78)
  local copies, waits for them, and re-layouts: 35 us -> 0 us
  Pallas kernels: 223 us -> 210 us
  other arithmetic: 10.8 us -> 0 us
    pallas_call x1, Pallas kernels: 223 us -> 206 us  [fast_shards(): pl.pallas_call(layers, out_shape=(jax.ShapeDtypeStruct((BLOCKS, shard, wi...]
    unnamed x37 -> x0, local copies, waits for them, and re-layouts: 10.3 us -> none
    slice x11 -> x0, local copies, waits for them, and re-layouts: 8.75 us -> none  [the longest x1 1.51 us: fast_shards(): vout[5:15]]
    pallas_call x0 -> x1, Pallas kernels: none -> 4.52 us  [fast_shards(): pl.pallas_call(unpack, out_shape=(out(micro, share, pairs, width), out(pa...]
    convert_element_type x4 -> x0, other arithmetic: 3.87 us -> none  [the longest x1 1.62 us: fast_shards(): ((pair_of[:, None] == image_of[None, :]) & (image_live > 0)[None, :]).ast...]
    reshape x8 -> x0, local copies, waits for them, and re-layouts: 3.63 us -> none  [the longest x1 1.62 us: fast_shards(): pjout.reshape(shard, 2, -1).transpose(1, 0, 2)]
    dynamic_slice x7 -> x0, local copies, waits for them, and re-layouts: 3.1 us -> none  [mine(): return lax.dynamic_slice_in_dim(array, group * half_micro, half_micro, 0)]
    pad x9 -> x0, local copies, waits for them, and re-layouts: 2.94 us -> none  [the longest x1 1.02 us: fast_shards(): jnp.pad(mine(image_embeds), ((0, 0), (0, 0), (0, IMAGE_PAD - images), (0,...]
where the time goes in v2:
time: 211 us
  Pallas kernels  210 us (100%)
    pallas_call x1, Pallas kernels, fast_shards(): pl.pallas_call(layers, out_shape=(jax.ShapeDtypeStruct((BLOCKS, shard, wi...  206 us
    pallas_call x1, Pallas kernels, fast_shards(): pl.pallas_call(unpack, out_shape=(out(micro, share, pairs, width), out(pa...  4.52 us

profile of v2, /device:TPU:0, one launch (start us, length us, event | category | flops | bytes accessed | tf_op | source)
XLA Modules:
  0.0 211.1 jit_solution(1633656223146707141)
XLA Ops:
  0.7 205.7 %shard_map.314 = (f32[7,96,768]{2,1,0:T(8,128)}, f32[2,40,768]{2,1,0:T(8,128)}, f32[2,40,768]{2,1,0:T(8,128)}, bf16[2,304,384]{2,1,0:T(8,128)(2,1)}, f32[96,512]...) custom-call(s32[2,4]{1,0:T(2,128)} %bitcast.15, bf16[3,96,192]{2,1,0:T(8,128)(2,1)} %arrays_0_.1, ...), custom_call_target="tpu_custom_call" | custom-call | tf_op jit(solution)/shard_map/pallas_call | solution.py:1691
  206.4 4.5 %shard_map.315 = (f32[4,10,2,768]{3,2,1,0:T(2,128)}, f32[2,4]{1,0:T(2,128)}, f32[4,10,2,768]{3,2,1,0:T(2,128)}, f32[4,145,2,192]{3,2,1,0:T(2,128)}, f32[3,96,192...) custom-call(f32[7,96,768]{2,1,0:T(8,128)} %get-tuple-element.41.wout, ...), custom_call_target="tpu_custom_call" | custom-call | tf_op jit(solution)/shard_map/pallas_call | solution.py:1713

commit v3 on v2

--- a/solution.py
+++ b/solution.py
@@ -610,7 +610,7 @@
 T_ATT, T_UP, T_DOWN, M_SELF, M_CROSS, M_UP, M_DOWN = range(7)
 BLOCKS = 7
 BACK_ORDER = (M_DOWN, M_UP, M_CROSS, M_SELF, T_DOWN, T_UP, T_ATT)
-SLOTS = 4
+SLOTS = 5
 IMAGE_PAD = 16
 NORMS = 5
 
@@ -665,7 +665,7 @@
     merge_qkv, merge_out, merge_up, merge_down, gains, offs, image_ids, projections, cot,
     wout, mout, tgout, imout, pjout, lossout, vout,
     G, PJ, H, XH, RSD, SQ, SK, SV, CQ, CK, CV, OA, PS, PC, PRE, ACT, XS, XR, ACC, DZ, DPRE, DQKV, DKV,
-    RC, R2, R1, RZ, BG, CT, MS, TG, IMO, IMS, IMR, IML, tmask, cmask, CG, CLS, DU, DUW, DPJ, PXF, PXS, PXR, LSR, MSB, MRX, V, VR, LS,
+    RC, R2, R1, RZ, BG, CT, MS, TG, IMO, IMS, IMR, IML, tmask, cmask, CG, CLS, DU, DUW, DPJ, TXS, TXR, PXF, PXS, PXR, LSR, MSB, MRX, V, VR, LS,
     img,
     load_s,
     z_s, z_r, s1_s, s1_r, s2_s, s2_r, sc_s, sc_r,
@@ -759,22 +759,24 @@
     def hop_1(k, q):
         part = G.at[k, q, y, x, c]
         return remote(
-            part, part, s1_s.at[k, q], s1_r.at[k, q], to_x if x_first(k, q) else to_y
+            part, part, s1_s.at[k, q, 0], s1_r.at[k, q, 0], to_x if x_first(k, q) else to_y
         )
 
     def hop_2(k, q):
         part = G.at[k, q, y, :, c] if x_first(k, q) else G.at[k, q, :, x, c]
         return remote(
-            part, part, s2_s.at[k, q], s2_r.at[k, q], to_y if x_first(k, q) else to_x
+            part, part, s2_s.at[k, q, 0], s2_r.at[k, q, 0], to_y if x_first(k, q) else to_x
         )
 
     def hop_c(k, q):
         part = G.at[k, q, :, :, c]
         return remote(part, part, sc_s.at[k, q], sc_r.at[k, q], to_c)
 
+    cuts = [pl.ds(0, width // 16), pl.ds(width // 16, width // 16)]
+
     own_proj = PJ.at[y, x, c]
-    p_1 = remote(own_proj, own_proj, s1_s.at[BLOCKS, 0], s1_r.at[BLOCKS, 0], to_x)
-    p_2 = remote(PJ.at[y, :, c], PJ.at[y, :, c], s2_s.at[BLOCKS, 0], s2_r.at[BLOCKS, 0], to_y)
+    p_1 = remote(own_proj, own_proj, s1_s.at[BLOCKS, 0, 0], s1_r.at[BLOCKS, 0, 0], to_x)
+    p_2 = remote(PJ.at[y, :, c], PJ.at[y, :, c], s2_s.at[BLOCKS, 0, 0], s2_r.at[BLOCKS, 0, 0], to_y)
     p_c = remote(PJ.at[:, :, c], PJ.at[:, :, c], sc_s.at[BLOCKS, 0], sc_r.at[BLOCKS, 0], to_c)
 
     def tick(j):
@@ -1048,23 +1050,27 @@
     sent_all()
     V[...] = jnp.zeros_like(V)
 
+    def slot(k):
+        return BACK_ORDER.index(k) % SLOTS
+
     def back_c(k, q):
-        slot = BACK_ORDER.index(k) % SLOTS
         return remote(
-            G.at[k, q, :, :, 1 - c], RC.at[slot, q], bc_s.at[k, q], bc_r.at[k, q], to_c
+            G.at[k, q, :, :, 1 - c], RC.at[slot(k), q], bc_s.at[k, q], bc_r.at[k, q], to_c
         )
 
     def back_2(k, q):
-        part = G.at[k, q, 1 - y, :, c] if x_first(k, q) else G.at[k, q, :, 1 - x, c]
-        return remote(
-            part, R2.at[k, q], b2_s.at[k, q], b2_r.at[k, q], to_y if x_first(k, q) else to_x
-        )
+        parts = [G.at[k, q, 1 - y, :, c, cuts[0]], G.at[k, q, :, 1 - x, c, cuts[1]]]
+        return [
+            remote(part, R2.at[k, q, h], b2_s.at[k, q, h], b2_r.at[k, q, h], (to_y, to_x)[h])
+            for h, part in enumerate(parts)
+        ]
 
     def back_1(k, q):
-        part = G.at[k, q, y, 1 - x, c] if x_first(k, q) else G.at[k, q, 1 - y, x, c]
-        return remote(
-            part, R1.at[k, q], b1_s.at[k, q], b1_r.at[k, q], to_x if x_first(k, q) else to_y
-        )
+        parts = [G.at[k, q, y, 1 - x, c, cuts[0]], G.at[k, q, 1 - y, x, c, cuts[1]]]
+        return [
+            remote(part, R1.at[k, q, h], b1_s.at[k, q, h], b1_r.at[k, q, h], (to_x, to_y)[h])
+            for h, part in enumerate(parts)
+        ]
 
     def back_z(k):
         return remote(G.at[k, 1, y, x, c], RZ.at[k], bz_s.at[k], bz_r.at[k], to_z2)
@@ -1072,37 +1078,36 @@
     def both(a, b):
         return (a.astype(F32) + b.astype(F32)).astype(BF)
 
-    def c_start(n):
-        for q in range(2):
-            back_c(BACK_ORDER[n], q).start()
-
-    def a_step(n):
+    def a_step(n, q):
         k = BACK_ORDER[n]
-        for q in range(2):
-            back_c(k, q).wait()
-            for a in range(2):
-                for b in range(2):
-                    G[k, q, a, b, c] = both(G[k, q, a, b, c], RC[n % SLOTS, q, a, b])
-            back_2(k, q).start()
-
-    def b_step(n):
+        back_c(k, q).wait()
+        for a in range(2):
+            for b in range(2):
+                G[k, q, a, b, c] = both(G[k, q, a, b, c], RC[slot(k), q, a, b])
+        for copy in back_2(k, q):
+            copy.start()
+
+    def b_step(n, q):
         k = BACK_ORDER[n]
-        for q in range(2):
-            back_2(k, q).wait()
-            for a in range(2):
-                if x_first(k, q):
-                    G[k, q, y, a, c] = both(G[k, q, y, a, c], R2[k, q, a])
-                else:
-                    G[k, q, a, x, c] = both(G[k, q, a, x, c], R2[k, q, a])
-            back_1(k, q).start()
-
-    def d_step(n):
+        for copy in back_2(k, q):
+            copy.wait()
+        for a in range(2):
+            G[k, q, y, a, c, cuts[0]] = both(G[k, q, y, a, c, cuts[0]], R2[k, q, 0, a])
+            G[k, q, a, x, c, cuts[1]] = both(G[k, q, a, x, c, cuts[1]], R2[k, q, 1, a])
+        for copy in back_1(k, q):
+            copy.start()
+
+    def d_step(n, q):
         k = BACK_ORDER[n]
-        back_1(k, 1).wait()
-        G[k, 1, y, x, c] = both(G[k, 1, y, x, c], R1[k, 1])
-        back_z(k).start()
-        back_1(k, 0).wait()
-        wout[k] = G[k, 0, y, x, c].astype(F32) + R1[k, 0].astype(F32)
+        for copy in back_1(k, q):
+            copy.wait()
+        for h in range(2):
+            if q == 1:
+                G[k, q, y, x, c, cuts[h]] = both(G[k, q, y, x, c, cuts[h]], R1[k, q, h])
+            else:
+                wout[k, cuts[h]] = G[k, q, y, x, c, cuts[h]].astype(F32) + R1[k, q, h].astype(F32)
+        if q == 1:
+            back_z(k).start()
 
     def e_step(n):
         k = BACK_ORDER[n]
@@ -1111,15 +1116,15 @@
 
     def norm_backward(e, grad):
         xhat = XH[e]
-        V[e : e + 1, :] = jnp.sum(grad * xhat, 0, keepdims=True)
-        V[2 * NORMS + e : 2 * NORMS + e + 1, :] = jnp.sum(grad, 0, keepdims=True)
+        V[0, e : e + 1, :] = jnp.sum(grad * xhat, 0, keepdims=True)
+        V[0, 2 * NORMS + e : 2 * NORMS + e + 1, :] = jnp.sum(grad, 0, keepdims=True)
         scaled = grad * gains[e : e + 1, :]
         first = jnp.mean(scaled, -1, keepdims=True)
         second = jnp.mean(scaled * xhat, -1, keepdims=True)
         grad = RSD[e] * (scaled - first - xhat * second)
         DZ[...] = grad
         rounded = grad.astype(BF)
-        V[NORMS + e : NORMS + e + 1, :] = jnp.sum(rounded.astype(F32), 0, keepdims=True)
+        V[0, NORMS + e : NORMS + e + 1, :] = jnp.sum(rounded.astype(F32), 0, keepdims=True)
         return rounded
 
     def keep_grad(k, q, lo, value):
@@ -1132,7 +1137,8 @@
         ACC[...] = jnp.zeros_like(ACC)
         turned = rounded.T
 
-        def part(q, carry):
+        def part(i, carry):
+            q = 1 - i
             grad = mm(rounded, weight(down, q, 0, width))
             keep_grad(down, q, 0, mm(turned, ACT[layer, q]))
             back_c(down, q).start()
@@ -1142,7 +1148,7 @@
             )
             grad = (grad * slope).astype(BF)
             DPRE[q] = grad
-            V[pl.ds(15 + 2 * q + layer, 1), :] = jnp.sum(grad.astype(F32), 0, keepdims=True)
+            V[1, pl.ds(2 * q + layer, 1), :] = jnp.sum(grad.astype(F32), 0, keepdims=True)
             ACC[...] += mm_nt(grad, weight(up, q, 0, width))
             return carry
 
@@ -1151,8 +1157,10 @@
     def feed_up_grad(up, e):
         turned = H[e].T
 
-        def part(q, carry):
+        def part(i, carry):
+            q = 1 - i
             keep_grad(up, q, 0, mm(turned, DPRE[q]))
+            back_c(up, q).start()
             return carry
 
         lax.fori_loop(0, 2, part, 0)
@@ -1168,17 +1176,18 @@
         return grad_queries.astype(BF), grad_keys.astype(BF), grad_values.astype(BF)
 
     def bias_sums(q, layer, grad_queries, grad_values):
-        V[pl.ds(19 + 6 * q + 2 * layer, 1), 0:local] = jnp.sum(
+        V[1, pl.ds(4 + 6 * q + 2 * layer, 1), 0:local] = jnp.sum(
             grad_queries.astype(F32), 0, keepdims=True
         )
-        V[pl.ds(20 + 6 * q + 2 * layer, 1), 0:local] = jnp.sum(
+        V[1, pl.ds(5 + 6 * q + 2 * layer, 1), 0:local] = jnp.sum(
             grad_values.astype(F32), 0, keepdims=True
         )
 
     def self_backward(k, layer, rounded):
         ACC[...] = jnp.zeros_like(ACC)
 
-        def part(q, carry):
+        def part(i, carry):
+            q = 1 - i
             grad_mixed = mm(rounded, weight(k, q, 3 * local, 4 * local)).astype(BF)
             parts = []
             for n in range(heads):
@@ -1205,7 +1214,8 @@
         turned = H[e].T
         turned_out = rounded.T
 
-        def part(q, carry):
+        def part(i, carry):
+            q = 1 - i
             keep_grad(
                 k,
                 q,
@@ -1214,6 +1224,7 @@
                     [mm(turned, DQKV[q]), mm(turned_out, OA[layer, q])], 1
                 ),
             )
+            back_c(k, q).start()
             return carry
 
         lax.fori_loop(0, 2, part, 0)
@@ -1221,7 +1232,8 @@
     def cross_backward(rounded):
         ACC[...] = jnp.zeros_like(ACC)
 
-        def part(q, carry):
+        def part(i, carry):
+            q = 1 - i
             grad_mixed = mm(rounded, weight(M_CROSS, q, 3 * local, 4 * local)).astype(BF)
             parts = []
             for n in range(heads):
@@ -1261,7 +1273,8 @@
         turned_out = rounded.T
         turned_image = img[...].T
 
-        def part(q, carry):
+        def part(i, carry):
+            q = 1 - i
             keep_grad(
                 M_CROSS,
                 q,
@@ -1275,6 +1288,7 @@
                     1,
                 ),
             )
+            back_c(M_CROSS, q).start()
             return carry
 
         lax.fori_loop(0, 2, part, 0)
@@ -1393,45 +1407,47 @@
     merged = settle_forward(4)
     rounded = norm_backward(4, DZ[...])
     feed_backward(M_UP, M_DOWN, 4, 1, rounded)
+    swap_start(5)
+    p_2.wait()
+    p_c.start()
+    feed_up_grad(M_UP, 4)
     MS[...] = merged.reshape(4, quarter, width)
-    swap_start(5)
-    feed_up_grad(M_UP, 4)
-    c_start(1)
-    a_step(0)
     mout[group] = MS[z]
     MSB[0] = MS[z2].astype(BF)
     merged_copy = remote(MSB.at[0], MRX.at[0], m_s.at[4], m_r.at[4], to_z2)
     text_copy = remote(MSB.at[1], MRX.at[1], m_s.at[8], m_r.at[8], to_z2)
     merged_copy.start()
-    p_2.wait()
-    p_c.start()
-    rounded = norm_backward(3, DZ[...] + swap_sum(5))
-    a_step(1)
-    cross_backward(rounded)
-    swap_start(6)
-    b_step(0)
-    IMS[...] = image_columns(z1, z3).astype(BF)
-    IMO[...] = image_columns(z, z2)
-    cross_grad(rounded)
-    c_start(2)
-    b_step(1)
-    rounded = norm_backward(2, DZ[...] + swap_sum(6))
-    a_step(2)
-    image_copy.start()
-    d_step(0)
-    self_backward(M_SELF, 1, rounded)
-    swap_start(7)
-    self_grad(M_SELF, 2, 1, rounded)
-    c_start(3)
-    d_step(1)
-    b_step(2)
-    a_step(3)
+    a_step(0, 1)
+    a_step(1, 1)
+    a_step(0, 0)
     p_c.wait()
     for copy in summary:
         copy.wait()
     contrast()
     pair_copy.start()
     loss_copy.start()
+    b_step(0, 1)
+    rounded = norm_backward(3, DZ[...] + swap_sum(5))
+    cross_backward(rounded)
+    swap_start(6)
+    a_step(1, 0)
+    b_step(1, 1)
+    IMS[...] = image_columns(z1, z3).astype(BF)
+    IMO[...] = image_columns(z, z2)
+    d_step(0, 1)
+    b_step(0, 0)
+    cross_grad(rounded)
+    a_step(2, 1)
+    b_step(1, 0)
+    d_step(1, 1)
+    rounded = norm_backward(2, DZ[...] + swap_sum(6))
+    self_backward(M_SELF, 1, rounded)
+    swap_start(7)
+    self_grad(M_SELF, 2, 1, rounded)
+    b_step(2, 1)
+    a_step(3, 1)
+    image_copy.start()
+    d_step(2, 1)
 
     proj_text = PJ[:, :, :, :, 0 : PJ.shape[-1] // 2].reshape(width, PJ.shape[-1] // 2)
     extra = mm_exact(DU[dp], proj_text.astype(F32), NT)
@@ -1442,73 +1458,99 @@
             place == n // pairs * share * pairs + n % pairs, extra[n : n + 1, :], 0.0
         )
     rounded = norm_backward(1, grad)
+    b_step(3, 1)
     feed_backward(T_UP, T_DOWN, 1, 0, rounded)
     swap_start(8)
-    d_step(2)
+    a_step(3, 0)
+    a_step(4, 1)
+    d_step(3, 1)
     feed_up_grad(T_UP, 1)
-    c_start(5)
-    b_step(3)
-    a_step(4)
+    a_step(4, 0)
+    d_step(0, 0)
     image_finish()
+    b_step(4, 1)
+    e_step(0)
+    b_step(4, 0)
+    a_step(5, 1)
+    d_step(1, 0)
+    a_step(2, 0)
+    d_step(4, 1)
     rounded = norm_backward(0, DZ[...] + swap_sum(8))
-    a_step(5)
-    e_step(0)
-    e_step(1)
     self_backward(T_ATT, 0, rounded)
-    swap_start(9)
-
-    stat_to = (to_c, to_x, to_y, to_z2)
+
+    MS[...] = ACC[...].reshape(4, quarter, width)
+    TXS[0] = MS[z1].astype(BF)
+    TXS[1] = MS[z3].astype(BF)
+    text_swap = remote(TXS, TXR, x_s.at[2], x_r.at[9], to_z1)
+    text_swap.start()
+    TG[...] = (DZ[...] + ACC[...]).reshape(4, quarter, width)
+
+    stat_from = (V.at[1 - c], V.at[c], V.at[c], V.at[c], V.at[c])
+    stat_to = (to_c, to_x, to_y, to_z2, to_c)
 
     def stat_copy(i):
-        return remote(V, VR.at[i], v_s.at[i], v_r.at[i], stat_to[i])
-
-    stat_copy(0).start()
-    d_step(3)
-    b_step(4)
-    self_grad(T_ATT, 0, 0, rounded)
-    c_start(6)
-    b_step(5)
-    a_step(6)
-    d_step(4)
-
-    grad = DZ[...] + swap_sum(9)
-    TG[...] = grad.reshape(4, quarter, width)
-    MSB[1] = TG[z2].astype(BF)
-    text_copy.start()
-    tgout[group] = TG[z]
+        return remote(stat_from[i], VR.at[i], v_s.at[i], v_r.at[i], stat_to[i])
+
     def stat_step(i):
         stat_copy(i).wait()
-        if i < 3:
-            V[...] = V[...] + VR[i]
+        known = VR[i]
+        if i == 3:
+            turned = jnp.concatenate(
+                [known[2:4], known[0:2], known[10:16], known[4:10]], 0
+            )
+            known = jnp.where(c == 0, known, turned)
+        if i < 4:
+            V[c] = V[c] + known
             stat_copy(i + 1).start()
-
+        else:
+            vout[c] = V[c]
+            vout[1 - c] = known
+
+    stat_copy(0).start()
+    d_step(4, 0)
+    self_grad(T_ATT, 0, 0, rounded)
+    b_step(5, 1)
     stat_step(0)
-    d_step(5)
+    e_step(1)
+    a_step(6, 1)
+    d_step(5, 1)
     stat_step(1)
-    b_step(6)
+    b_step(2, 0)
+    e_step(4)
+    b_step(6, 1)
+    b_step(3, 0)
+    a_step(5, 0)
+    stat_step(2)
+    a_step(6, 0)
+    d_step(6, 1)
+    text_swap.wait()
+    tgout[group] = TG[z] + TXR[0].astype(F32)
+    MSB[1] = (TG[z2] + TXR[1].astype(F32)).astype(BF)
+    text_copy.start()
+    d_step(2, 0)
+    b_step(5, 0)
+    b_step(6, 0)
+    d_step(3, 0)
+    e_step(3)
     e_step(2)
-    stat_step(2)
-    e_step(3)
-    e_step(4)
-    d_step(6)
     stat_step(3)
-    vout[0:15, :] = V[0:15, :] + VR[3, 0:15, :]
-    vout[16:18, :] = V[15:17, :] + VR[3, 17:19, :]
-    vout[24:30, :] = V[19:25, :] + VR[3, 25:31, :]
-    e_step(5)
     pair_copy.wait()
     loss_copy.wait()
     pjout[...] = PXF[...] + PXR[...].astype(F32)
     lossout[group] = LS[dp]
     lossout[1 - group] = LSR[...]
+    merged_copy.wait()
+    mout[1 - group] = MRX[0].astype(F32)
     image_last.wait()
+    stat_step(4)
+    d_step(6, 0)
+    d_step(5, 0)
+    e_step(5)
+    e_step(6)
     text_copy.wait()
     tgout[1 - group] = MRX[1].astype(F32)
-    merged_copy.wait()
-    mout[1 - group] = MRX[0].astype(F32)
+    swap(7).wait_send()
     swap(8).wait_send()
-    swap(9).wait_send()
-    e_step(6)
 
 
 def unpack(
@@ -1562,10 +1604,10 @@
     half = pjout.shape[1] // 2
     projections[0] = pjout[:, :half]
     projections[1] = pjout[:, half:]
-    gains[...] = vout[0:5, :]
-    offs[...] = vout[5:15, :]
-    up_bias[...] = vout[16:18, :]
-    head_bias[...] = vout[24:30, 0:local]
+    gains[...] = vout[0, 0:5, :]
+    offs[...] = vout[0, 5:15, :]
+    up_bias[...] = vout[1, 0:2, :]
+    head_bias[...] = vout[1, 4:10, 0:local]
 
 
 def fast_shards(
@@ -1645,8 +1687,8 @@
         buf(2, rows, 3 * local),
         buf(2, half_micro * image_rows, 2 * local),
         buf(SLOTS, 2, 2, 2, shard, width),
-        buf(BLOCKS, 2, 2, shard, width),
-        buf(BLOCKS, 2, shard, width),
+        buf(BLOCKS, 2, 2, 2, shard // 2, width),
+        buf(BLOCKS, 2, 2, shard // 2, width),
         buf(BLOCKS, shard, width),
         buf(2, 8, width, dtype=F32),
         buf(model_parts, half_micro, share, pairs, width),
@@ -1663,30 +1705,34 @@
         buf(data_parts, 8, proj_width // 2, dtype=F32),
         buf(data_parts, 8, proj_width // 2, dtype=F32),
         buf(data_parts, shard, proj_width // 2, dtype=F32),
+        buf(2, quarter, width),
+        buf(2, quarter, width),
         buf(shard, proj_width, dtype=F32),
         buf(shard, proj_width),
         buf(shard, proj_width),
         buf(8, 128, dtype=F32),
         buf(2, quarter, width),
         buf(2, quarter, width),
-        buf(32, width, dtype=F32),
-        buf(4, 32, width, dtype=F32),
+        buf(2, 16, width, dtype=F32),
+        buf(5, 16, width, dtype=F32),
         buf(data_parts, 8, 128, dtype=F32),
         buf(half_micro * image_rows, width),
         sem(LOADS),
         sem(BLOCKS),
         sem(BLOCKS),
-        *[sem(BLOCKS + 1, 2) for _ in range(6)],
-        *[sem(BLOCKS, 2) for _ in range(6)],
+        *[sem(BLOCKS + 1, 2, 2) for _ in range(4)],
+        *[sem(BLOCKS + 1, 2) for _ in range(2)],
+        *[sem(BLOCKS, 2, 2) for _ in range(4)],
+        *[sem(BLOCKS, 2) for _ in range(2)],
         *[sem(BLOCKS) for _ in range(2)],
-        sem(2),
+        sem(3),
         sem(2 * NORMS),
         sem(10),
         sem(10),
         sem(data_parts - 1),
         sem(data_parts - 1),
-        sem(4),
-        sem(4),
+        sem(5),
+        sem(5),
     ]
     packed = pl.pallas_call(
         layers,
@@ -1697,7 +1743,7 @@
             jax.ShapeDtypeStruct((groups, image_rows, half_micro * local), BF),
             jax.ShapeDtypeStruct((shard, proj_width), F32),
             jax.ShapeDtypeStruct((groups, 8, 128), F32),
-            jax.ShapeDtypeStruct((32, width), F32),
+            jax.ShapeDtypeStruct((2, 16, width), F32),
         ),
         in_specs=[pl.BlockSpec(memory_space=pltpu.SMEM)] + [pl.BlockSpec(memory_space=pl.ANY)] * LOADS,
         out_specs=(vmem,) * 7,

time: 211 us -> 204 us (0.967)
  Pallas kernels: 210 us -> 203 us
    pallas_call x1, Pallas kernels: 206 us -> 198 us  [fast_shards(): pl.pallas_call(layers, out_shape=(jax.ShapeDtypeStruct((BLOCKS, shard, wi...]
where the time goes in v3:
time: 204 us
  Pallas kernels  203 us (100%)
    pallas_call x1, Pallas kernels, fast_shards(): pl.pallas_call(layers, out_shape=(jax.ShapeDtypeStruct((BLOCKS, shard, wi...  198 us
    pallas_call x1, Pallas kernels, fast_shards(): pl.pallas_call(unpack, out_shape=(out(micro, share, pairs, width), out(pa...  4.52 us

profile of v3, /device:TPU:0, one launch (start us, length us, event | category | flops | bytes accessed | tf_op | source)
XLA Modules:
  0.0 203.8 jit_solution(18290767973154488754)
XLA Ops:
  0.7 198.4 %shard_map.314 = (f32[7,96,768]{2,1,0:T(8,128)}, f32[2,40,768]{2,1,0:T(8,128)}, f32[2,40,768]{2,1,0:T(8,128)}, bf16[2,304,384]{2,1,0:T(8,128)(2,1)}, f32[96,512]...) custom-call(s32[2,4]{1,0:T(2,128)} %bitcast.15, bf16[3,96,192]{2,1,0:T(8,128)(2,1)} %arrays_0_.1, ...), custom_call_target="tpu_custom_call" | custom-call | tf_op jit(solution)/shard_map/pallas_call | solution.py:1737
  199.1 4.5 %shard_map.315 = (f32[4,10,2,768]{3,2,1,0:T(2,128)}, f32[2,4]{1,0:T(2,128)}, f32[4,10,2,768]{3,2,1,0:T(2,128)}, f32[4,145,2,192]{3,2,1,0:T(2,128)}, f32[3,96,192...) custom-call(f32[7,96,768]{2,1,0:T(8,128)} %get-tuple-element.41.wout, ...), custom_call_target="tpu_custom_call" | custom-call | tf_op jit(solution)/shard_map/pallas_call | solution.py:1759
